TPU v7x, 128 devices: a whole 4x4x4 slice. The times are simulated.
128 devices in a mesh: dp: 4 (over x), ctx: 32 (over y, z, core).
Axes of the slice: x: 4, y: 4, z: 4, core: 2. Of those that a mesh axis runs over, the one named last changes fastest.
Arguments:
- queries: bfloat16 [8192, 1024], P('ctx'), may hold values from -12 to 12
- keys: bfloat16 [8192, 128], P('ctx'), may hold values from -5 to 5
- values: bfloat16 [8192, 128], P('ctx'), may hold values from -5 to 5
- out_grad: bfloat16 [8192, 1024], P('ctx'), may hold values from -5 to 5
- segment_ids: int32 [8192], replicated, may hold values from 0 to 3, never falling along the last dimension, each value on 1 to 7168 neighbouring positions
Outputs:
- attn_out: bfloat16 [8192, 1024], P('ctx', 'dp')
- grad_q: bfloat16 [8192, 1024], P('ctx', 'dp')
- grad_k: bfloat16 [8192, 128], P(('dp', 'ctx'))
- grad_v: bfloat16 [8192, 128], P(('dp', 'ctx'))
Inputs may be any that keep to these rules, and one draw needn't show every extreme that they name: `segment_ids`: document numbers never fall along the tokens; each document is a run of positions, the longest exactly 7168.
All inputs are finite; a program needn't handle non-finite values.
Results may differ from a plain program's by a relative error of at most 0.04.
Values may be sent and summed in bfloat16 or wider, within the bound.
A program may use at most 64 MiB of HBM per device.

v0:
```python
import math

import jax
import jax.numpy as jnp
from jax import lax
from jax.sharding import PartitionSpec as P

KEY_TILE = 512


NEG_START = -1e30


def merged(array, axis, combine):
    everything = jax.tree.map(lambda part: lax.all_gather(part, axis), array)
    initial = jax.tree.map(lambda part: part[0], everything)

    def step(k, so_far):
        return combine(so_far, jax.tree.map(lambda part: part[k], everything))

    return lax.fori_loop(1, lax.axis_size(axis), step, initial)


def on_device(queries, keys, values, out_grad, segment_ids):
    rows = queries.shape[0]
    width = keys.shape[1]
    heads = queries.shape[1] // width
    seq = segment_ids.shape[0]
    scale = width ** (-0.5)
    ctx_index = lax.axis_index("ctx")
    dp_index = lax.axis_index("dp")
    dp_count = lax.axis_size("dp")
    query_pos = ctx_index * rows + jnp.arange(rows, dtype=jnp.int32)
    seg_q = lax.dynamic_slice_in_dim(segment_ids, ctx_index * rows, rows, 0)
    query_h = queries.reshape(rows, heads, width).transpose(1, 0, 2)
    grad_h = out_grad.reshape(rows, heads, width).transpose(1, 0, 2)

    def owned(key_start):
        tile = key_start // KEY_TILE
        return tile % dp_count == dp_index

    def over_piece(carry, piece, step_fn):
        count_rows = piece[0].shape[0]
        sub = math.gcd(count_rows, KEY_TILE)

        def one_tile(index, state):
            key_start = index * sub
            key_b = lax.dynamic_slice_in_dim(piece[0], index * sub, sub, 0)
            val_b = lax.dynamic_slice_in_dim(piece[1], index * sub, sub, 0)
            key_pos = key_start + jnp.arange(sub, dtype=jnp.int32)
            seg_k = lax.dynamic_slice_in_dim(segment_ids, key_start, sub, 0)
            allowed = (seg_q[:, None] == seg_k[None, :]) & (key_pos[None, :] <= query_pos[:, None])
            needed = owned(key_start) & jnp.any(allowed)
            return lax.cond(
                needed,
                lambda inner: step_fn(inner, key_b, val_b, key_start, allowed),
                lambda inner: inner,
                state,
            )

        return lax.fori_loop(0, count_rows // sub, one_tile, carry)

    def forward_step(state, key_b, val_b, key_start, allowed):
        rowmax, total, accum = state
        scores = (
            jnp.einsum("hqd,kd->hqk", query_h, key_b, preferred_element_type=jnp.float32) * scale
        )
        scores = jnp.where(allowed[None], scores, -jnp.inf)
        new_max = jnp.maximum(rowmax, jnp.max(scores, axis=-1))
        expd = jnp.exp(scores - new_max[..., None])
        factor = jnp.exp(rowmax - new_max)
        total = total * factor + jnp.sum(expd, axis=-1)
        weighted = jnp.einsum(
            "hqk,kd->hqd", expd.astype(jnp.bfloat16), val_b, preferred_element_type=jnp.float32
        )
        accum = accum * factor[..., None] + weighted
        return (new_max, total, accum)

    start_state = (
        jnp.full((heads, rows), NEG_START, jnp.float32),
        jnp.zeros((heads, rows), jnp.float32),
        jnp.zeros((heads, rows, width), jnp.float32),
    )
    partial_value = over_piece(
        start_state,
        (
            lax.all_gather(keys, "ctx", axis=0, tiled=True),
            lax.all_gather(values, "ctx", axis=0, tiled=True),
        ),
        forward_step,
    )

    def combine(first, second):
        top = jnp.maximum(first[0], second[0])
        scale_a = jnp.exp(first[0] - top)
        scale_b = jnp.exp(second[0] - top)
        return (
            top,
            first[1] * scale_a + second[1] * scale_b,
            first[2] * scale_a[..., None] + second[2] * scale_b[..., None],
        )

    rowmax, total, accum = merged(
        (partial_value[0], partial_value[1], partial_value[2]), "dp", combine
    )
    output_bf = (accum / total[..., None]).astype(jnp.bfloat16)
    columns = heads * width // dp_count
    out_rows = output_bf.transpose(1, 0, 2).reshape(rows, heads * width)
    attn_out = lax.dynamic_slice_in_dim(out_rows, dp_index * columns, columns, 1)
    lse = rowmax + jnp.log(total)
    delta = jnp.sum(grad_h.astype(jnp.float32) * output_bf.astype(jnp.float32), axis=-1)

    def backward_step(state, key_b, val_b, key_start, allowed):
        grad_query, key_terms, val_terms = state
        sub = key_b.shape[0]
        scores = (
            jnp.einsum("hqd,kd->hqk", query_h, key_b, preferred_element_type=jnp.float32) * scale
        )
        probs = jnp.where(allowed[None], jnp.exp(scores - lse[..., None]), 0.0)
        val_block = jnp.einsum(
            "hqk,hqd->kd", probs.astype(jnp.bfloat16), grad_h, preferred_element_type=jnp.float32
        )
        dprobs = jnp.einsum("hqd,kd->hqk", grad_h, val_b, preferred_element_type=jnp.float32)
        dscores = (probs * (dprobs - delta[..., None])).astype(jnp.bfloat16)
        grad_query = (
            grad_query
            + jnp.einsum("hqk,kd->hqd", dscores, key_b, preferred_element_type=jnp.float32) * scale
        )
        key_block = (
            jnp.einsum("hqk,hqd->kd", dscores, query_h, preferred_element_type=jnp.float32) * scale
        )
        key_terms = lax.dynamic_update_slice_in_dim(
            key_terms,
            lax.dynamic_slice_in_dim(key_terms, key_start, sub, 0) + key_block,
            key_start,
            0,
        )
        val_terms = lax.dynamic_update_slice_in_dim(
            val_terms,
            lax.dynamic_slice_in_dim(val_terms, key_start, sub, 0) + val_block,
            key_start,
            0,
        )
        return (grad_query, key_terms, val_terms)

    empty_terms = jnp.zeros((seq, width), jnp.float32)
    grad_start = (jnp.zeros((heads, rows, width), jnp.float32), empty_terms, empty_terms)
    grad_query, key_terms, val_terms = over_piece(
        grad_start,
        (
            lax.all_gather(keys, "ctx", axis=0, tiled=True),
            lax.all_gather(values, "ctx", axis=0, tiled=True),
        ),
        backward_step,
    )
    query_rows = grad_query.transpose(1, 0, 2).reshape(rows, heads * width)
    grad_q = lax.psum_scatter(
        query_rows.astype(jnp.bfloat16), "dp", scatter_dimension=1, tiled=True
    )
    grad_keys, grad_vals = (
        lax.psum_scatter(key_terms, ("dp", "ctx"), scatter_dimension=0, tiled=True),
        lax.psum_scatter(val_terms, ("dp", "ctx"), scatter_dimension=0, tiled=True),
    )
    return (attn_out, grad_q, grad_keys.astype(jnp.bfloat16), grad_vals.astype(jnp.bfloat16))


def solution(mesh):
    return jax.shard_map(
        on_device,
        mesh=mesh,
        in_specs=(P("ctx", None), P("ctx", None), P("ctx", None), P("ctx", None), P()),
        out_specs=(P("ctx", "dp"), P("ctx", "dp"), P(("dp", "ctx"), None), P(("dp", "ctx"), None)),
        check_vma=False,
    )
```

profile of v0, /device:TPU:1, one launch (start us, length us, event | category | flops | bytes accessed | tf_op | source)
XLA Modules:
  0.0 1612.2 jit_solution(7030302946751426523)
XLA Ops:
  8.7 1.2 copy.25
  11.0 46.9 %all-gather.7.cloned.1.call-done = bf16[8192,128]{1,0:T(8,128)(2,1)} async-done(((bf16[256,128]{1,0:T(8,128)(2,1)}), bf16[8192,128]{1,0:T(8,128)(2,1)}) %all-gather.7.cloned.1.call-update) | async-done | bytes 2097168 | tf_op jit(solution)/shard_map/all_gather | solution.py:87
  57.9 45.5 %all-gather.9.cloned.1.call-done = bf16[8192,128]{1,0:T(8,128)(2,1)} async-done(((bf16[256,128]{1,0:T(8,128)(2,1)}), bf16[8192,128]{1,0:T(8,128)(2,1)}) %all-gather.9.cloned.1.call-update) | async-done | bytes 2097168 | tf_op jit(solution)/shard_map/all_gather | solution.py:88
  103.5 43.0 %while.60 = (s32[]{:T(128)}, f32[8,256]{1,0:T(8,128)S(1)}, f32[8,256]{1,0:T(8,128)S(1)}, f32[8,256,128]{2,1,0:T(8,128)S(1)}, s32[]{:T(128)}, /*index=5*/s32[256]...) while((s32[]{:T(128)}, f32[8,256]{1,0:T(8,128)S(1)}, ...), condition=%wide.region_6.7_spmd.clone, body=%wide.region_0.6_spmd.clone.sunk | while | flops 549458688 | bytes 16136819 | solution.py:61
  105.9 5.0 conditional.6
  106.0 1.6 fusion.6
  108.5 2.4 fusion.10
  146.6 1.0 copy-done
  147.8 1.0 copy.31
  148.9 9.0 all-gather
  157.9 9.0 all-gather.1
  166.9 42.4 %all-gather.11.cloned.1.call-done = f32[32,256,128]{2,1,0:T(8,128)} async-done(((f32[8,256,128]{2,1,0:T(8,128)}), f32[32,256,128]{2,1,0:T(8,128)}) %all-gather.11.cloned.1.call-update) | async-done | bytes 4194320 | tf_op jit(solution)/shard_map/all_gather | solution.py:15
  209.3 1.3 slice.17
  210.6 6.5 while.59
  210.7 2.1 fusion.70
  212.9 2.1 fusion.70
  215.1 2.1 fusion.70
  217.5 1.0 multiply_reduce_fusion
  218.6 2.2 broadcast_in_dim.76.clone
  220.8 2.2 broadcast_in_dim.76
  223.1 48.9 %while.61 = (s32[]{:T(128)}, f32[8,256,128]{2,1,0:T(8,128)S(1)}, f32[8192,128]{1,0:T(8,128)}, f32[8192,128]{1,0:T(8,128)}, s32[]{:T(128)}, /*index=5*/s32[256]{0...) while((s32[]{:T(128)}, f32[8,256,128]{2,1,0:T(8,128)S(1)}, ...), condition=%wide.region_14.15_spmd.clone, body=%wide.region_10.14_spmd.clone.sunk | while | flops 1353908992 | bytes 24943828 | solution.py:61
  223.8 0.9 fusion.72
  225.4 10.7 conditional.7
  225.4 1.6 fusion.45
  227.0 2.3 fusion.25
  229.3 1.8 fusion.30
  231.1 2.6 fusion.40
  233.7 2.4 fusion.36
  236.9 0.9 fusion.72
  239.3 0.9 fusion.72
  241.7 0.9 fusion.72
  244.1 0.9 fusion.72
  246.5 0.9 fusion.72
  248.9 0.9 fusion.72
  251.3 0.9 fusion.72
  253.7 0.9 fusion.72
  256.1 0.9 fusion.72
  258.5 0.9 fusion.72
  260.8 0.9 fusion.72
  263.2 0.9 fusion.72
  270.4 0.9 fusion.72
  272.7 0.9 copy_bitcast_fusion
  273.6 0.9 constant_dynamic-slice_fusion
  275.3 666.7 %reduce-scatter.8.cloned.1.call-done = f32[64,128]{1,0:T(8,128)} async-done(((f32[8192,128]{1,0:T(8,128)}), f32[64,128]{1,0:T(8,128)}) %reduce-scatter.8.cloned.1.call-update) | async-done | bytes 32784 | tf_op jit(solution)/shard_map/reduce_scatter | solution.py:162
  941.9 1.4 convert_element_type.66
  943.3 639.0 %reduce-scatter.6.cloned.1.call-done = f32[64,128]{1,0:T(8,128)} async-done(((f32[8192,128]{1,0:T(8,128)}), f32[64,128]{1,0:T(8,128)}) %reduce-scatter.6.cloned.1.call-update) | async-done | bytes 32784 | tf_op jit(solution)/shard_map/reduce_scatter | solution.py:161
  1582.3 1.4 convert_element_type.65
  1583.6 21.7 %reduce-scatter.4.cloned.1.call-done = bf16[256,256]{1,0:T(8,128)(2,1)} async-done(((bf16[256,1024]{1,0:T(8,128)(2,1)}), bf16[256,256]{1,0:T(8,128)(2,1)}) %reduce-scatter.4.cloned.1.call-update) | async-done | bytes 131088 | tf_op jit(solution)/shard_map/reduce_scatter | solution.py:157
  (180 shorter events, 46.4 us)
Async XLA Ops:
  7.2 50.8 %all-gather.7.cloned.1.call-start = ((), (), s32[]{:S(2)}) async-start(), calls=%async_computation.3 | async-start | bytes 2162688 | tf_op jit(solution)/shard_map/all_gather | solution.py:87
  7.9 95.6 %all-gather.9.cloned.1.call-start = ((), (), s32[]{:S(2)}) async-start(), calls=%async_computation.4 | async-start | bytes 2162688 | tf_op jit(solution)/shard_map/all_gather | solution.py:88
  8.6 200.7 %all-gather.11.cloned.1.call-start = ((), (), s32[]{:S(2)}) async-start(), calls=%async_computation.8 | async-start | bytes 5242880 | tf_op jit(solution)/shard_map/all_gather | solution.py:15
  103.5 44.1 %copy-start.1 = (bf16[256,1024]{1,0:T(8,128)(2,1)S(1)}, bf16[256,1024]{1,0:T(8,128)(2,1)}, u32[]{:S(2)}) copy-start(bf16[256,1024]{1,0:T(8,128)(2,1)} %param.18) | copy-start | bytes 1572868
  146.6 1.0 copy-start
  147.6 794.4 %reduce-scatter.8.cloned.1.call-start = ((), (), s32[]{:S(2)}) async-start(), calls=%async_computation.7 | async-start | bytes 4227072 | tf_op jit(solution)/shard_map/reduce_scatter | solution.py:162
  218.6 4.5 copy-start.2
  272.0 1310.2 %reduce-scatter.6.cloned.1.call-start = ((), (), s32[]{:S(2)}) async-start(), calls=%async_computation.6 | async-start | bytes 4227072 | tf_op jit(solution)/shard_map/reduce_scatter | solution.py:161
  272.6 1332.7 %reduce-scatter.4.cloned.1.call-start = ((), (), s32[]{:S(2)}) async-start(), calls=%async_computation.5 | async-start | bytes 655360 | tf_op jit(solution)/shard_map/reduce_scatter | solution.py:157
Sparse Core Ops, SparseCore 0:
  10.3 47.6 all-gather.6
  60.2 43.2 all-gather.8
  147.7 61.6 all-gather.10
  272.1 669.7 reduce-scatter.7
  944.2 637.9 reduce-scatter.5
  1585.1 20.1 reduce-scatter.3
where the time goes:
time: 1620 us; the launch traced here: 1610 us
  waiting for transfers between devices  1460 us (90%)
  other arithmetic  40.4 us (2%)
  local copies, waits for them, and re-layouts  36.9 us (2%)
  loops' own time  23.4 us (1%)
  blocking collectives  18 us (1%)
    reduce_scatter x1, waiting for transfers between devices, on_device(): lax.psum_scatter(val_terms, ('dp', 'ctx'), scatter_dimension=0, tiled=True)  667 us
    reduce_scatter x1, waiting for transfers between devices, on_device(): lax.psum_scatter(key_terms, ('dp', 'ctx'), scatter_dimension=0, tiled=True)  639 us
    all_gather x1, waiting for transfers between devices, on_device(): lax.all_gather(keys, 'ctx', axis=0, tiled=True)  46.9 us
    all_gather x1, waiting for transfers between devices, on_device(): lax.all_gather(values, 'ctx', axis=0, tiled=True)  45.5 us
    all_gather x1, waiting for transfers between devices, merged(): everything = jax.tree.map(lambda part: lax.all_gather(part, axis), array)  42.4 us
  transfers between devices with their start and end apart: 6, of which 6 were waited for; matrix products, arithmetic and copies ran while one was open for 1% of the time, Pallas kernels for 0%

commit v1 on v0

v1 whole, which is shorter than its diff:
```python
import math

import jax
import jax.numpy as jnp
from jax import lax
from jax.experimental import pallas as pl
from jax.experimental.pallas import tpu as pltpu
from jax.sharding import PartitionSpec as P

F32 = jnp.float32
BF16 = jnp.bfloat16
MESH = pl.DeviceIdType.MESH

N = 4
ROWS = 256
BLOCKS = 32
WIDTH = 128
SEQ = ROWS * BLOCKS
TILE = 512
TILES = 17
NEG = -1e30
PIECES = (
    (0, 0, 48, "xyz"),
    (1, 0, 48, "yzx"),
    (0, 48, 16, "zxy"),
    (1, 48, 16, "zxy"),
)


def dot(a, b):
    return lax.dot_general(a, b, (((1,), (0,)), ((), ())), preferred_element_type=F32)


def kernel(
    seg_ref, q_hbm, k_ref, v_ref, g_hbm,
    out_ref, dq_ref, dk_ref, dv_ref,
    kall, vall, qbuf, gbuf, s_buf, e_buf,
    qa, gpa, gp, mx, tot, o_t, dq_t, rng, dkv, part, sib, comb,
    r1a, r1b, r1c, r1d, r2a, r2b, r2c, r2d, r3a, r3b, r3c, r3d, d2a, d2b, d2c, d2d, d3a, d3b, d3c, d3d,
    obuf, orecv,
    load_sem, ag_send, ag_recv, pair_send, pair_recv, out_send, out_recv, sib_send, sib_recv, rs_send, rs_recv,
):
    p = lax.axis_index("dp")
    c = lax.axis_index("ctx")
    core = c % 2
    z = (c // 2) % N
    y = c // (2 * N)
    at = dict(x=p, y=y, z=z)

    def index(y_, z_, core_):
        return (y_ * N + z_) * 2 + core_

    def peer(axis, d):
        there = dict(at)
        there[axis] = (at[axis] + d) % N
        return (there["x"], index(there["y"], there["z"], core))

    sibling = (p, index(y, z, 1 - core))
    partner = (p, BLOCKS - 1 - c)
    upper = (c >= BLOCKS // 2).astype(jnp.int32)
    own_unit = 1 - upper
    lo = jnp.minimum(c, BLOCKS - 1 - c)
    hi = BLOCKS - 1 - lo
    n_hi = (hi + 2) // 2

    barrier = pltpu.get_barrier_semaphore()
    friends = [peer(a, d) for a in "xyz" for d in (1, 2, 3)] + [sibling, partner]
    for there in friends:
        pl.semaphore_signal(barrier, inc=1, device_id=there, device_id_type=MESH)
    my_head = 2 * p + upper
    pair_head = 2 * p + 1 - upper

    def head_cols(head):
        return pl.ds(pl.multiple_of(head * WIDTH, WIDTH), WIDTH)

    loads = [
        pltpu.make_async_copy(src.at[:, head_cols(my_head)], buf.at[own_unit], load_sem.at[i])
        for i, (src, buf) in enumerate(((q_hbm, qbuf), (g_hbm, gbuf)))
    ]
    for copy in loads:
        copy.start()
    kall[c] = k_ref[...]
    vall[c] = v_ref[...]
    pl.semaphore_wait(barrier, len(friends))

    def remote(src, dst, send, recv, there):
        return pltpu.make_async_remote_copy(
            src_ref=src, dst_ref=dst, send_sem=send, recv_sem=recv, device_id=there, device_id_type=MESH
        )

    pair_copies = [
        remote(src.at[:, head_cols(pair_head)], buf.at[own_unit], pair_send.at[i], pair_recv.at[i], partner)
        for i, (src, buf) in enumerate(((q_hbm, qbuf), (g_hbm, gbuf)))
    ]

    started = []
    count = [0, 0]

    def push(which, block, there):
        buf = (kall, vall)[which]
        copy = remote(
            buf.at[block], buf.at[block], ag_send.at[which, count[which]], ag_recv.at[which, block], there
        )
        count[which] += 1
        copy.start()
        started.append(copy)

    def arrived(which, block):
        buf = (kall, vall)[which]
        remote(
            buf.at[block], buf.at[block], ag_send.at[which, 0], ag_recv.at[which, block], sibling
        ).wait_recv()

    first, second = ("y", "z"), ("z", "y")
    for d in (1, 3, 2):
        for which in (0, 1):
            push(which, c, peer(first[which], d))
    for which in (0, 1):
        push(which, c, sibling)
    for copy in pair_copies:
        copy.start()
    for d in (1, 3, 2):
        for which in (0, 1):
            push(which, c, peer(second[which], d))
    from_y = lambda d: index((y - d) % N, z, core)
    from_z = lambda d: index(y, (z - d) % N, core)
    for d in (1, 3, 2):
        for which in (0, 1):
            block = from_y(d) if which == 0 else from_z(d)
            arrived(which, block)
            for d2 in (1, 3, 2):
                push(which, block, peer(second[which], d2))
            push(which, block, sibling)
    for d in (1, 3, 2):
        for d2 in (0, 1, 3, 2):
            for which in (0, 1):
                if which == 0:
                    block = index((y - d2) % N, (z - d) % N, core)
                else:
                    block = index((y - d) % N, (z - d2) % N, core)
                arrived(which, block)
                push(which, block, sibling)
    for dy in range(N):
        for dz in range(N):
            for which in (0, 1):
                arrived(which, index((y + dy) % N, (z + dz) % N, 1 - core))
    for copy in loads:
        copy.wait()
    for copy in pair_copies:
        copy.wait_recv()

    scale = WIDTH**-0.5
    seg = seg_ref[...]
    starts = [
        jnp.sum((seg < doc).astype(jnp.int32), axis=(0, 1), keepdims=True) for doc in (1, 2, 3)
    ]
    lane = lax.broadcasted_iota(jnp.int32, (1, WIDTH), 1)
    for unit, block in ((0, hi), (1, lo)):
        for half in range(2):
            ids = seg_ref[pl.ds(2 * block + half, 1), :]
            start = jnp.where(
                ids == 0, 0, jnp.where(ids == 1, starts[0], jnp.where(ids == 2, starts[1], starts[2]))
            )
            rng[unit, 0, :, half * WIDTH : (half + 1) * WIDTH] = start
            rng[unit, 1, :, half * WIDTH : (half + 1) * WIDTH] = block * ROWS + half * WIDTH + lane
        scaled = qbuf[unit].astype(F32).T * (scale * math.log2(math.e))
        high = scaled.astype(BF16)
        qa[unit, :WIDTH] = high
        qa[unit, WIDTH:] = (scaled - high.astype(F32)).astype(BF16)
    mx[...] = jnp.full_like(mx, NEG)
    tot[...] = jnp.zeros_like(tot)
    o_t[...] = jnp.zeros_like(o_t)
    dq_t[...] = jnp.zeros_like(dq_t)

    def zero(i, carry):
        dkv[0, i] = jnp.zeros((ROWS, WIDTH), F32)
        dkv[1, i] = jnp.zeros((ROWS, WIDTH), F32)
        return carry

    lax.fori_loop(0, BLOCKS, zero, 0)

    per = TILE // ROWS
    row = lax.broadcasted_iota(jnp.int32, (TILE, ROWS), 0)

    def place(t):
        unit = (t >= n_hi).astype(jnp.int32)
        return unit, t - unit * n_hi

    def tile_of(buf, kt):
        return buf[pl.ds(kt * per, per)].reshape(TILE, WIDTH)

    def scores_step(t, carry):
        unit, kt = place(t)
        k = tile_of(kall, kt)
        s = dot(jnp.concatenate([k, k], axis=1), qa[unit])
        key = row + kt * TILE
        s = jnp.where((key >= rng[unit, 0]) & (key <= rng[unit, 1]), s, NEG)
        s_buf[t] = s
        mx[unit] = jnp.maximum(mx[unit], jnp.max(s.reshape(TILE // 8, 8, ROWS), axis=0))
        return carry

    lax.fori_loop(0, TILES, scores_step, 0)
    for unit in (0, 1):
        mx[unit] = jnp.broadcast_to(jnp.max(mx[unit], axis=0, keepdims=True), (8, ROWS))

    def weights_step(t, carry):
        unit, kt = place(t)
        e = jnp.exp2(s_buf[t] - mx[unit, 0:1])
        tot[unit] = tot[unit] + jnp.sum(e.reshape(TILE // 8, 8, ROWS), axis=0)
        e = e.astype(BF16)
        e_buf[t] = e
        o_t[unit] = o_t[unit] + dot(tile_of(vall, kt).T, e)
        return carry

    lax.fori_loop(0, TILES, weights_step, 0)
    for unit in (0, 1):
        inv = 1.0 / jnp.sum(tot[unit], axis=0, keepdims=True)
        out_t = o_t[unit] * inv
        obuf[0, unit] = out_t.T.astype(BF16)
        grad = (gbuf[unit].astype(F32).T * inv).astype(BF16)
        grad_f = grad.astype(F32)
        gp[unit] = grad_f.T.astype(BF16)
        delta = -jnp.sum(grad_f * out_t, axis=0, keepdims=True)
        d1 = delta.astype(BF16).astype(F32)
        d2 = (delta - d1).astype(BF16).astype(F32)
        d3 = delta - d1 - d2
        sub = lax.broadcasted_iota(jnp.int32, (WIDTH, ROWS), 0)
        extra = jnp.where(sub == 0, d1, jnp.where(sub == 1, d2, jnp.where(sub == 2, d3, 0.0)))
        gpa[unit, :WIDTH] = grad
        gpa[unit, WIDTH:] = extra.astype(BF16)
    out_copies = [remote(obuf.at[0, 1 - own_unit], orecv.at[0], out_send.at[0], out_recv.at[0], partner)]
    out_copies[0].start()

    ones = jnp.ones((TILE, WIDTH), BF16)

    def grads_step(t, carry):
        unit, kt = place(t)
        e = e_buf[t]
        k = tile_of(kall, kt)
        dp = dot(jnp.concatenate([tile_of(vall, kt), ones], axis=1), gpa[unit])
        ds = (e.astype(F32) * dp).astype(BF16)
        at_ = pl.ds(kt * per, per)
        dkv[1, at_] = dkv[1, at_] + dot(e, gp[unit]).reshape(per, ROWS, WIDTH)
        dkv[0, at_] = dkv[0, at_] + dot(ds, qbuf[unit]).reshape(per, ROWS, WIDTH)
        dq_t[unit] = dq_t[unit] + dot(k.T, ds)
        return carry

    lax.fori_loop(0, TILES, grads_step, 0)
    for unit in (0, 1):
        obuf[1, unit] = (dq_t[unit] * scale).T.astype(BF16)
    out_copies.append(remote(obuf.at[1, 1 - own_unit], orecv.at[1], out_send.at[1], out_recv.at[1], partner))
    out_copies[1].start()

    def to_half(i, carry):
        both = dkv[:, i].reshape(2, 2, 2, 64, WIDTH)
        for which, factor in ((0, scale), (1, 1.0)):
            part[which, pl.ds(2 * i, 2)] = (both[which] * factor).astype(BF16)
        return carry

    lax.fori_loop(0, BLOCKS, to_half, 0)
    sib_copies = [
        remote(part.at[i, :, 1 - core], sib.at[i], sib_send.at[i], sib_recv.at[i], sibling) for i in (0, 1)
    ]
    for copy in sib_copies:
        copy.start()
    for copy in sib_copies:
        copy.wait_recv()

    def add_core(i, carry):
        for which in (0, 1):
            total = part[which, i, core].astype(F32) + sib[which, i].astype(F32)
            comb[which, i // 16, (i // 4) % 4, i % 4] = total.astype(BF16)
        return carry

    lax.fori_loop(0, 64, add_core, 0)

    def cut(ref, axes, axis, i, rows=None):
        return ref.at[tuple(i if a == axis else slice(None) for a in axes) + ((rows, slice(None)) if rows else ())]

    recvs = ((r1a, r2a, r3a), (r1b, r2b, r3b), (r1c, r2c, r3c), (r1d, r2d, r3d))
    sums = ((d2a, d3a), (d2b, d3b), (d2c, d3c), (d2d, d3d))
    rs_copies = {}

    def launch(i, phase, src, axes, rows=None):
        axis = PIECES[i][3][phase]
        for d in (1, 3, 2):
            copy = remote(
                cut(src, axes, axis, (at[axis] + d) % N, rows), recvs[i][phase].at[d - 1],
                rs_send.at[i, phase, d - 1], rs_recv.at[i, phase, d - 1], peer(axis, d),
            )
            copy.start()
            rs_copies[i, phase, d] = copy

    def settle(i, phase):
        for d in (1, 3, 2):
            rs_copies[i, phase, d].wait_recv()

    order = (0, 1, 2, 3)
    for i in order:
        which, first_row, n, axes = PIECES[i]
        launch(i, 0, comb.at[which], "xyz", slice(first_row, first_row + n))
    for i in order:
        which, first_row, n, axes = PIECES[i]
        settle(i, 0)
        left = [a for a in "xyz" if a != axes[0]]

        def add_first(j, carry, i=i, which=which, first_row=first_row, n=n, axes=axes, left=left):
            spot = dict(zip(left, (j // N, j % N)))
            spot[axes[0]] = at[axes[0]]
            total = comb[which, spot["x"], spot["y"], spot["z"], first_row : first_row + n].astype(F32)
            for d in range(N - 1):
                total = total + recvs[i][0][d, j // N, j % N].astype(F32)
            sums[i][0][j // N, j % N] = total.astype(BF16)
            return carry

        lax.fori_loop(0, N * N, add_first, 0)
        launch(i, 1, sums[i][0], left)
    for i in order:
        which, first_row, n, axes = PIECES[i]
        settle(i, 1)
        left = [a for a in "xyz" if a != axes[0]]
        for j in range(N):
            spot = {axes[1]: at[axes[1]], axes[2]: j}
            total = sums[i][0][spot[left[0]], spot[left[1]]].astype(F32)
            for d in range(N - 1):
                total = total + recvs[i][1][d, j].astype(F32)
            sums[i][1][j] = total.astype(BF16)
        launch(i, 2, sums[i][1], axes[2])
    for i in order:
        which, first_row, n, axes = PIECES[i]
        settle(i, 2)
        total = sums[i][1][at[axes[2]]].astype(F32)
        for d in range(N - 1):
            total = total + recvs[i][2][d].astype(F32)
        (dk_ref, dv_ref)[which][first_row : first_row + n] = total.astype(BF16)

    mine = pl.ds(pl.multiple_of(upper * WIDTH, WIDTH), WIDTH)
    other = pl.ds(pl.multiple_of((1 - upper) * WIDTH, WIDTH), WIDTH)
    for i, ref in enumerate((out_ref, dq_ref)):
        ref[:, mine] = obuf[i, own_unit]
        out_copies[i].wait_recv()
        ref[:, other] = orecv[i]
    for copy in started + pair_copies + out_copies + sib_copies + list(rs_copies.values()):
        copy.wait_send()


def on_device(queries, keys, values, out_grad, segment_ids):
    vmem = pl.BlockSpec(memory_space=pltpu.VMEM)
    hbm = pl.BlockSpec(memory_space=pl.ANY)
    dma = pltpu.SemaphoreType.DMA
    sizes = [n for _, _, n, _ in PIECES]
    scratch = [
        pltpu.VMEM((BLOCKS, ROWS, WIDTH), BF16),
        pltpu.VMEM((BLOCKS, ROWS, WIDTH), BF16),
        pltpu.VMEM((2, ROWS, WIDTH), BF16),
        pltpu.VMEM((2, ROWS, WIDTH), BF16),
        pltpu.VMEM((TILES, TILE, ROWS), F32),
        pltpu.VMEM((TILES, TILE, ROWS), BF16),
        pltpu.VMEM((2, 2 * WIDTH, ROWS), BF16),
        pltpu.VMEM((2, 2 * WIDTH, ROWS), BF16),
        pltpu.VMEM((2, ROWS, WIDTH), BF16),
        pltpu.VMEM((2, 8, ROWS), F32),
        pltpu.VMEM((2, 8, ROWS), F32),
        pltpu.VMEM((2, WIDTH, ROWS), F32),
        pltpu.VMEM((2, WIDTH, ROWS), F32),
        pltpu.VMEM((2, 2, 1, ROWS), jnp.int32),
        pltpu.VMEM((2, BLOCKS, ROWS, WIDTH), F32),
        pltpu.VMEM((2, 64, 2, 64, WIDTH), BF16),
        pltpu.VMEM((2, 64, 64, WIDTH), BF16),
        pltpu.VMEM((2, N, N, N, 64, WIDTH), BF16),
    ]
    scratch += [pltpu.VMEM((N - 1, N, N, n, WIDTH), BF16) for n in sizes]
    scratch += [pltpu.VMEM((N - 1, N, n, WIDTH), BF16) for n in sizes]
    scratch += [pltpu.VMEM((N - 1, n, WIDTH), BF16) for n in sizes]
    scratch += [pltpu.VMEM((N, N, n, WIDTH), BF16) for n in sizes]
    scratch += [pltpu.VMEM((N, n, WIDTH), BF16) for n in sizes]
    scratch += [
        pltpu.VMEM((2, 2, ROWS, WIDTH), BF16),
        pltpu.VMEM((2, ROWS, WIDTH), BF16),
        dma((2,)),
        dma((2, BLOCKS)),
        dma((2, BLOCKS)),
        dma((2,)), dma((2,)),
        dma((2,)), dma((2,)),
        dma((2,)), dma((2,)),
        dma((4, 3, 3)), dma((4, 3, 3)),
    ]
    tokens = jax.ShapeDtypeStruct((ROWS, 2 * WIDTH), BF16)
    terms = jax.ShapeDtypeStruct((64, WIDTH), BF16)
    return pl.pallas_call(
        kernel,
        out_shape=(tokens, tokens, terms, terms),
        in_specs=[vmem, hbm, vmem, vmem, hbm],
        out_specs=(vmem, vmem, vmem, vmem),
        scratch_shapes=scratch,
        compiler_params=pltpu.CompilerParams(
            collective_id=0, has_side_effects=True, vmem_limit_bytes=56 * 1024 * 1024
        ),
    )(segment_ids.reshape(SEQ // WIDTH, WIDTH), queries, keys, values, out_grad)


def solution(mesh):
    return jax.shard_map(
        on_device,
        mesh=mesh,
        in_specs=(P("ctx", None), P("ctx", None), P("ctx", None), P("ctx", None), P()),
        out_specs=(P("ctx", "dp"), P("ctx", "dp"), P(("dp", "ctx"), None), P(("dp", "ctx"), None)),
        check_vma=False,
    )
```

time: 1620 us -> 79.3 us (0.05)
  waiting for transfers between devices: 1460 us -> 0 us
  Pallas kernels: 0 us -> 73.7 us
  other arithmetic: 40.4 us -> 0 us
  local copies, waits for them, and re-layouts: 36.9 us -> 3.65 us
  loops' own time: 23.4 us -> 0 us
  blocking collectives: 18 us -> 0 us
    reduce_scatter x3 -> x0, waiting for transfers between devices: 1330 us -> none  [the longest x1 667 us: on_device(): lax.psum_scatter(val_terms, ('dp', 'ctx'), scatter_dimension=0, tiled=True)]
    all_gather x3 -> x0, waiting for transfers between devices: 135 us -> none  [the longest x1 46.9 us: on_device(): lax.all_gather(keys, 'ctx', axis=0, tiled=True)]
    pallas_call x0 -> x1, Pallas kernels: none -> 73.7 us  [on_device(): pl.pallas_call(kernel, out_shape=(tokens, tokens, terms, terms), in_specs...]
    reduce_or x32 -> x0, other arithmetic: 28.3 us -> none  [one_tile(): needed = owned(key_start) & jnp.any(allowed)]
    dynamic_slice x34 -> x0, local copies, waits for them, and re-layouts: 26.2 us -> none  [the longest x32 24.5 us: one_tile(): seg_k = lax.dynamic_slice_in_dim(segment_ids, key_start, sub, 0)]
    another operation x35 -> x0, loops' own time: 23.4 us -> none  [the longest x2 22.9 us: over_piece(): return lax.fori_loop(0, count_rows // sub, one_tile, carry)]
    all_gather x2 -> x0, blocking collectives: 18 us -> none  [merged(): everything = jax.tree.map(lambda part: lax.all_gather(part, axis), array)]
  transfers between devices with their start and end apart: 6 -> 0, of which waited for: 6 -> 0; matrix products, arithmetic and copies ran while one was open for 1% -> 0% of each run, Pallas kernels for 0% -> 0%
where the time goes in v1:
time: 79.3 us; the launch traced here: 78.1 us
  Pallas kernels  73.7 us (93%)
  local copies, waits for them, and re-layouts  3.65 us (5%)
    pallas_call x1, Pallas kernels, on_device(): pl.pallas_call(kernel, out_shape=(tokens, tokens, terms, terms), in_specs...  73.7 us
    unnamed x10, local copies, waits for them, and re-layouts  3.65 us

profile of v1, /device:TPU:1, one launch (start us, length us, event | category | flops | bytes accessed | tf_op | source)
XLA Modules:
  0.0 78.1 jit_solution(16330731117590940873)
XLA Ops:
  0.6 73.7 %shard_map.84 = (bf16[256,256]{1,0:T(8,128)(2,1)}, bf16[256,256]{1,0:T(8,128)(2,1)}, bf16[64,128]{1,0:T(8,128)(2,1)}, bf16[64,128]{1,0:T(8,128)(2,1)}) custom-call(s32[64,128]{1,0:T(8,128)} %bitcast.1, bf16[256,1024]{1,0:T(8,128)(2,1)} %q_hbm.1, bf16[256,128]{1,0:T(8,128)(2,1)} %k_ref.1, bf16[256,128]{1,0:T(8,128)(2,1)} %v_ref.1, bf16[256,1024]{1,0:T(8,128)(2,1)} %g_hbm.1), custom_call_target="tpu_custom_call" | custom-call | tf_op jit(solution)/shard_map/pallas_call | solution.py:390
  74.4 0.0 copy-start
  74.4 1.6 %copy.13 = bf16[256,256]{1,0:T(8,128)(2,1)} copy(bf16[256,256]{1,0:T(8,128)(2,1)} %get-tuple-element.8) | data formatting | bytes 262144
  76.0 0.0 copy-done
  76.0 0.0 copy-start.2
  76.0 0.7 copy.14
  76.7 0.1 copy-done.2
  76.7 0.0 copy-start.1
  76.7 0.6 copy.15
  77.3 0.1 copy-done.1
  77.4 0.6 copy.16
Async XLA Ops:
  74.4 1.6 %copy-start = (bf16[256,256]{1,0:T(8,128)(2,1)S(1)}, bf16[256,256]{1,0:T(8,128)(2,1)}, u32[]{:S(2)}) copy-start(bf16[256,256]{1,0:T(8,128)(2,1)} %get-tuple-element.9) | copy-start | bytes 393220
  76.0 0.7 copy-start.2
  76.7 0.7 copy-start.1

commit v2 on v0

v2 whole, which is shorter than its diff:
```python
import math

import jax
import jax.numpy as jnp
from jax import lax
from jax.experimental import pallas as pl
from jax.experimental.pallas import tpu as pltpu
from jax.sharding import PartitionSpec as P

F32 = jnp.float32
BF16 = jnp.bfloat16
MESH = pl.DeviceIdType.MESH

N = 4
CHIPS = N * N
ROWS = 256
PAIR = 2 * ROWS
WIDTH = 128
SEQ = PAIR * CHIPS
GROUP = 64
TILES = CHIPS + 1
NEG = -1e30


def dot(a, b):
    return lax.dot_general(a, b, (((1,), (0,)), ((), ())), preferred_element_type=F32)


def kernel(
    seg_hbm, q_hbm, k_hbm, v_hbm, g_hbm,
    out_hbm, dq_hbm, dk_hbm, dv_hbm,
    seg_ref, kall, vall, qbuf, gbuf, s_buf, e_buf,
    qa, gt, gpa, gp, mx, tot, o_t, dq_t, o_x, dq_x, st, st_x, rng, dkv,
    part, r1, d2, r2, d3, r3, final, obuf, orecv,
    load_sem, ag_send, ag_recv, q_send, q_recv, st_send, st_recv, mix_send, mix_recv, out_send, out_recv,
    rs_send, rs_recv, store_sem,
):
    p = lax.axis_index("dp")
    c = lax.axis_index("ctx")
    core = c % 2
    z = (c // 2) % N
    y = c // (2 * N)
    chip = c // 2
    at = dict(x=p, y=y, z=z)

    def peer(axis, d):
        there = dict(at)
        there[axis] = (at[axis] + d) % N
        return (there["x"], (there["y"] * N + there["z"]) * 2 + core)

    def chip_at(dy, dz):
        return ((y + N - dy) % N) * N + (z + N - dz) % N

    sibling = (p, 2 * chip + 1 - core)
    partner = (p, 2 * (CHIPS - 1 - chip) + core)
    upper = (chip >= CHIPS // 2).astype(jnp.int32)
    own = 1 - upper
    lo = jnp.minimum(chip, CHIPS - 1 - chip)
    hi = CHIPS - 1 - lo
    my_head = 2 * p + upper
    pair_head = 2 * p + 1 - upper

    def head_cols(head):
        return pl.ds(pl.multiple_of(head * WIDTH, WIDTH), WIDTH)

    barrier = pltpu.get_barrier_semaphore()
    friends = [peer(a, d) for a in "xyz" for d in (1, 2, 3)] + [sibling, partner]
    for there in friends:
        pl.semaphore_signal(barrier, inc=1, device_id=there, device_id_type=MESH)
    loads = [
        pltpu.make_async_copy(src, dst, load_sem.at[i])
        for i, (src, dst) in enumerate(
            (
                (k_hbm.at[:, core], kall.at[chip, core]),
                (v_hbm.at[:, core], vall.at[chip, core]),
                (q_hbm.at[:, head_cols(my_head)], qbuf.at[own, core]),
                (g_hbm.at[:, head_cols(my_head)], gbuf.at[own, core]),
                (seg_hbm, seg_ref),
            )
        )
    ]
    for copy in loads:
        copy.start()

    started = []

    def remote(src, dst, send, recv, there):
        return pltpu.make_async_remote_copy(
            src_ref=src, dst_ref=dst, send_sem=send, recv_sem=recv, device_id=there, device_id_type=MESH
        )

    def go(copy):
        copy.start()
        started.append(copy)
        return copy

    count = [0, 0]
    whole = (kall, vall)

    def next_send(which):
        count[which] += 1
        return ag_send.at[which, count[which] - 1]

    def push(which, block, part_of, there):
        spot = whole[which].at[block, part_of]
        go(remote(spot, spot, next_send(which), ag_recv.at[which, block, part_of], there))

    def arrived(which, block, part_of):
        spot = whole[which].at[block, part_of]
        remote(spot, spot, ag_send.at[which, 0], ag_recv.at[which, block, part_of], sibling).wait_recv()

    def push_mine(which):
        for axis in "yz":
            for d in (1, 3, 2):
                push(which, chip, core, peer(axis, d))

    def push_siblings(which):
        arrived(which, chip, 1 - core)
        for axis in "zy":
            for d in (1, 3, 2):
                push(which, chip, 1 - core, peer(axis, d))

    def relay(which):
        for d in (1, 3, 2):
            block = chip_at(d, 0)
            arrived(which, block, core)
            for d2 in (1, 3, 2):
                push(which, block, core, peer("z", d2))
            block = chip_at(0, d)
            arrived(which, block, 1 - core)
            for d2 in (1, 3, 2):
                push(which, block, 1 - core, peer("y", d2))

    def share_rows(i):
        src, buf = ((q_hbm, qbuf), (g_hbm, gbuf))[i]
        go(remote(src.at[:, head_cols(pair_head)], buf.at[own, core], q_send.at[i, 0], q_recv.at[i, 0], partner))
        mine = buf.at[own, core]
        loads[2 + i].wait()
        go(remote(mine, mine, q_send.at[i, 1], q_recv.at[i, 1], sibling))

    def pass_rows(i):
        buf = (qbuf, gbuf)[i]
        theirs = buf.at[1 - own, core]
        remote(theirs, theirs, q_send.at[i, 0], q_recv.at[i, 0], partner).wait_recv()
        go(remote(theirs, theirs, q_send.at[i, 2], q_recv.at[i, 2], sibling))
        for slot in (1, 2):
            spot = buf.at[own if slot == 1 else 1 - own, 1 - core]
            remote(spot, spot, q_send.at[i, slot], q_recv.at[i, slot], sibling).wait_recv()

    pl.semaphore_wait(barrier, len(friends))
    for which, src in ((0, k_hbm), (1, v_hbm)):
        go(
            remote(
                src.at[:, 1 - core], whole[which].at[chip, core],
                next_send(which), ag_recv.at[which, chip, core], sibling,
            )
        )
    loads[0].wait()
    push_mine(0)
    share_rows(0)
    push_siblings(0)
    share_rows(1)
    relay(0)
    loads[1].wait()
    push_mine(1)
    push_siblings(1)

    scale = WIDTH**-0.5
    loads[4].wait()
    seg = seg_ref[...]
    starts = [jnp.sum((seg < doc).astype(jnp.int32), axis=(0, 1), keepdims=True) for doc in (1, 2, 3)]
    lane = lax.broadcasted_iota(jnp.int32, (1, WIDTH), 1)
    for g, block in ((0, hi), (1, lo)):
        for i in range(PAIR // WIDTH):
            ids = seg_ref[pl.ds(block * (PAIR // WIDTH) + i, 1), :]
            start = jnp.where(
                ids == 0, 0, jnp.where(ids == 1, starts[0], jnp.where(ids == 2, starts[1], starts[2]))
            )
            rng[g, 0, :, i * WIDTH : (i + 1) * WIDTH] = start
            rng[g, 1, :, i * WIDTH : (i + 1) * WIDTH] = block * PAIR + i * WIDTH + lane
    mx[...] = jnp.full_like(mx, NEG)
    tot[...] = jnp.zeros_like(tot)
    o_t[...] = jnp.zeros_like(o_t)
    dq_t[...] = jnp.zeros_like(dq_t)
    pass_rows(0)
    for g in (0, 1):
        for r in (0, 1):
            cols = slice(r * ROWS, (r + 1) * ROWS)
            scaled = qbuf[g, r].astype(F32).T * (scale * math.log2(math.e))
            high = scaled.astype(BF16)
            qa[g, :WIDTH, cols] = high
            qa[g, WIDTH:, cols] = (scaled - high.astype(F32)).astype(BF16)

    row = lax.broadcasted_iota(jnp.int32, (ROWS, PAIR), 0)
    token = row + GROUP * (row // GROUP) + GROUP * core

    def slot_of(g, j):
        return j + g * (hi + 1)

    def rows_of(buf, j):
        return buf[j].reshape(ROWS, WIDTH)

    def fold(op, values):
        return op(values.reshape(ROWS // 8, 8, PAIR), axis=0)

    def scores_step(g, j):
        k = rows_of(kall, j)
        s = dot(jnp.concatenate([k, k], axis=1), qa[g])
        key = token + j * PAIR
        s = jnp.where((key >= rng[g, 0]) & (key <= rng[g, 1]), s, NEG)
        s_buf[slot_of(g, j)] = s
        mx[g] = jnp.maximum(mx[g], fold(jnp.max, s))

    def weights_step(g, j):
        t = slot_of(g, j)
        e = jnp.exp2(s_buf[t] - mx[g, 0:1])
        tot[g] = tot[g] + fold(jnp.sum, e)
        e = e.astype(BF16)
        e_buf[t] = e
        o = dot(rows_of(vall, j).T, e)
        for r in (0, 1):
            o_t[g, r] = o_t[g, r] + o[:, r * ROWS : (r + 1) * ROWS]

    def both_groups(step, j):
        for g, last in ((0, hi), (1, lo)):

            @pl.when(j <= last)
            def _(g=g):
                step(g, j)

    def over_row(which, step):
        both_groups(step, chip)

        def one(dz, carry):
            j = chip_at(0, dz)
            arrived(which, j, core)
            both_groups(step, j)
            return carry

        lax.fori_loop(1, N, one, 0)

    def over_rest(which, step):
        def one_row(dy, carry):
            j = chip_at(dy, 0)
            arrived(which, j, 1 - core)
            both_groups(step, j)

            def one(dz, inner):
                j = chip_at(dy, dz)
                arrived(which, j, core)
                arrived(which, j, 1 - core)
                both_groups(step, j)
                return inner

            lax.fori_loop(1, N, one, 0)
            return carry

        lax.fori_loop(1, N, one_row, 0)

    over_row(0, scores_step)
    relay(1)
    over_rest(0, scores_step)

    for g in (0, 1):
        mx[g] = jnp.broadcast_to(jnp.max(mx[g], axis=0, keepdims=True), (8, PAIR))
    pass_rows(1)
    for g in (0, 1):
        for r in (0, 1):
            gt[g, :, r * ROWS : (r + 1) * ROWS] = gbuf[g, r].astype(F32).T
    over_row(1, weights_step)
    over_rest(1, weights_step)

    for g in (0, 1):
        st[g, 0:1] = mx[g, 0:1]
        st[g, 1:2] = jnp.sum(tot[g], axis=0, keepdims=True)
        o = jnp.concatenate([o_t[g, 0], o_t[g, 1]], axis=1)
        st[g, 2:3] = jnp.sum(gt[g] * o, axis=0, keepdims=True)
        st[g, 3:8] = jnp.zeros((5, PAIR), F32)
    go(remote(st, st_x, st_send, st_recv, sibling)).wait_recv()
    sub = lax.broadcasted_iota(jnp.int32, (WIDTH, PAIR), 0)
    for g in (0, 1):
        top = jnp.maximum(st[g, 0:1], st_x[g, 0:1])
        here, there = jnp.exp2(st[g, 0:1] - top), jnp.exp2(st_x[g, 0:1] - top)
        inv = 1.0 / (here * st[g, 1:2] + there * st_x[g, 1:2])
        factor = here * inv
        delta = -(here * st[g, 2:3] + there * st_x[g, 2:3]) * inv * factor
        for r in (0, 1):
            o_t[g, r] = o_t[g, r] * factor[:, r * ROWS : (r + 1) * ROWS]
        grad = gt[g] * factor
        gpa[g, :WIDTH] = grad.astype(BF16)
        gp[g] = grad.T.astype(BF16)
        d1 = delta.astype(BF16).astype(F32)
        d2_ = (delta - d1).astype(BF16).astype(F32)
        extra = jnp.where(sub == 0, d1, jnp.where(sub == 1, d2_, jnp.where(sub == 2, delta - d1 - d2_, 0.0)))
        gpa[g, WIDTH:] = extra.astype(BF16)
    go(remote(o_t.at[:, 1 - core], o_x, mix_send.at[0], mix_recv.at[0], sibling))

    out_copies, stores = [], []

    def finish_rows(i):
        acc, other = ((o_t, o_x), (dq_t, dq_x))[i]
        remote(acc.at[:, core], other, mix_send.at[i], mix_recv.at[i], sibling).wait_recv()
        for g in (0, 1):
            total = acc[g, core] + other[g]
            if i == 1:
                total = total * scale
            obuf[i, g] = total.T.astype(BF16)
        out_copies.append(go(remote(obuf.at[i, 1 - own], orecv.at[i], out_send.at[i], out_recv.at[i], partner)))
        cols = pl.ds(pl.multiple_of(upper * WIDTH, WIDTH), WIDTH)
        store(obuf.at[i, own], (out_hbm, dq_hbm)[i].at[:, cols], i)

    def store(src, dst, i):
        stores.append(pltpu.make_async_copy(src, dst, store_sem.at[i]))
        stores[-1].start()

    def finish_partner_rows(i):
        out_copies[i].wait_recv()
        cols = pl.ds(pl.multiple_of((1 - upper) * WIDTH, WIDTH), WIDTH)
        store(orecv.at[i], (out_hbm, dq_hbm)[i].at[:, cols], 2 + i)

    ones = jnp.ones((ROWS, WIDTH), BF16)

    def grads_step(g, j):
        e = e_buf[slot_of(g, j)]
        k = rows_of(kall, j)
        dp = dot(jnp.concatenate([rows_of(vall, j), ones], axis=1), gpa[g])
        ds = (e.astype(F32) * dp).astype(BF16)
        terms = (dot(ds, qbuf[g].reshape(PAIR, WIDTH)), dot(e, gp[g]))
        for which in (0, 1):
            dkv[which, j] = terms[which] if g == 0 else dkv[which, j] + terms[which]
        dq = dot(k.T, ds)
        for r in (0, 1):
            dq_t[g, r] = dq_t[g, r] + dq[:, r * ROWS : (r + 1) * ROWS]

    rs_copies = {}

    def launch(phase, which, q, axis, src_of, dst_of):
        for d in (1, 3, 2):
            rs_copies[phase, which, q, d] = go(
                remote(
                    src_of((at[axis] + d) % N), dst_of(d - 1),
                    rs_send.at[phase, which, q, d - 1], rs_recv.at[phase, which, q, d - 1], peer(axis, d),
                )
            )

    def settle(phase, which, q):
        for d in (1, 3, 2):
            rs_copies[phase, which, q, d].wait_recv()

    def total_of(first, ref):
        total = first.astype(F32)
        for d in range(N - 1):
            total = total + ref[d].astype(F32)
        return total

    def first_phase(q):
        launch(0, 0, q, "y", lambda i: part.at[0, q, i], lambda s: r1.at[0, q, s])
        launch(0, 1, q, "z", lambda i: part.at[1, q, :, i], lambda s: r1.at[1, q, s])

    def second_phase(q):
        for which, axis in ((0, "z"), (1, "y")):
            settle(0, which, q)
            mine = part[0, q, y] if which == 0 else part[1, q, :, z]
            d2[which, q] = total_of(mine, r1.at[which, q]).astype(BF16)
            launch(1, which, q, axis, lambda i: d2.at[which, q, i], lambda s: r2.at[which, q, s])

    for q in reversed(range(N)):
        first, end = N * q, N * (q + 1)
        hi_end = jnp.clip(hi + 1, first, end)

        def hi_step(j, carry):
            grads_step(0, j)
            return carry

        def zero(j, carry):
            for which in (0, 1):
                dkv[which, j] = jnp.zeros((ROWS, WIDTH), F32)
            return carry

        def lo_step(j, carry):
            grads_step(1, j)
            return carry

        def round_off(j, carry):
            for which, by in ((0, scale), (1, 1.0)):
                part[which, q, j - first] = (dkv[which, j] * by).astype(BF16).reshape(N, GROUP, WIDTH)
            return carry

        lax.fori_loop(first, hi_end, hi_step, 0)
        lax.fori_loop(hi_end, end, zero, 0)
        if q < 2:
            lax.fori_loop(first, jnp.clip(lo + 1, first, end), lo_step, 0)
        lax.fori_loop(first, end, round_off, 0)
        first_phase(q)
        if q == 3:
            finish_rows(0)
        if q < 2:
            second_phase(q + 2)
    go(remote(dq_t.at[:, 1 - core], dq_x, mix_send.at[1], mix_recv.at[1], sibling))
    second_phase(1)
    finish_rows(1)
    second_phase(0)
    finish_partner_rows(0)
    for q in reversed(range(N)):
        for which, mine in ((0, z), (1, y)):
            settle(1, which, q)
            d3[which, q] = total_of(d2[which, q, mine], r2.at[which, q]).astype(BF16)
    for which in (0, 1):
        launch(2, which, 0, "x", lambda i: d3.at[which, i], lambda s: r3.at[which, s])
    finish_partner_rows(1)
    for which in (0, 1):
        settle(2, which, 0)
        final[which] = total_of(d3[which, p], r3.at[which]).astype(BF16)
        store(final.at[which], (dk_hbm, dv_hbm)[which], 4 + which)
    for copy in started:
        copy.wait_send()
    for copy in stores:
        copy.wait()


def on_device(queries, keys, values, out_grad, segment_ids):
    hbm = pl.BlockSpec(memory_space=pl.ANY)
    dma = pltpu.SemaphoreType.DMA
    vmem = pltpu.VMEM
    scratch = [
        vmem((SEQ // WIDTH, WIDTH), jnp.int32),
        vmem((CHIPS, 2, 2, GROUP, WIDTH), BF16),
        vmem((CHIPS, 2, 2, GROUP, WIDTH), BF16),
        vmem((2, 2, ROWS, WIDTH), BF16),
        vmem((2, 2, ROWS, WIDTH), BF16),
        vmem((TILES, ROWS, PAIR), F32),
        vmem((TILES, ROWS, PAIR), BF16),
        vmem((2, 2 * WIDTH, PAIR), BF16),
        vmem((2, WIDTH, PAIR), F32),
        vmem((2, 2 * WIDTH, PAIR), BF16),
        vmem((2, PAIR, WIDTH), BF16),
        vmem((2, 8, PAIR), F32),
        vmem((2, 8, PAIR), F32),
        vmem((2, 2, WIDTH, ROWS), F32),
        vmem((2, 2, WIDTH, ROWS), F32),
        vmem((2, WIDTH, ROWS), F32),
        vmem((2, WIDTH, ROWS), F32),
        vmem((2, 8, PAIR), F32),
        vmem((2, 8, PAIR), F32),
        vmem((2, 2, 1, PAIR), jnp.int32),
        vmem((2, CHIPS, ROWS, WIDTH), F32),
        vmem((2, N, N, N, GROUP, WIDTH), BF16),
        vmem((2, N, N - 1, N, GROUP, WIDTH), BF16),
        vmem((2, N, N, GROUP, WIDTH), BF16),
        vmem((2, N, N - 1, GROUP, WIDTH), BF16),
        vmem((2, N, GROUP, WIDTH), BF16),
        vmem((2, N - 1, GROUP, WIDTH), BF16),
        vmem((2, GROUP, WIDTH), BF16),
        vmem((2, 2, ROWS, WIDTH), BF16),
        vmem((2, ROWS, WIDTH), BF16),
        dma((5,)),
        dma((2, 32)),
        dma((2, CHIPS, 2)),
        dma((2, 3)),
        dma((2, 3)),
        dma,
        dma,
        dma((2,)),
        dma((2,)),
        dma((2,)),
        dma((2,)),
        dma((3, 2, N, N - 1)),
        dma((3, 2, N, N - 1)),
        dma((6,)),
    ]
    tokens = jax.ShapeDtypeStruct((ROWS, 2 * WIDTH), BF16)
    terms = jax.ShapeDtypeStruct((GROUP, WIDTH), BF16)
    return pl.pallas_call(
        kernel,
        out_shape=(tokens, tokens, terms, terms),
        in_specs=[hbm] * 5,
        out_specs=(hbm,) * 4,
        scratch_shapes=scratch,
        compiler_params=pltpu.CompilerParams(
            collective_id=0, has_side_effects=True, vmem_limit_bytes=56 * 1024 * 1024
        ),
    )(
        segment_ids.reshape(SEQ // WIDTH, WIDTH),
        queries,
        keys.reshape(2, 2, GROUP, WIDTH),
        values.reshape(2, 2, GROUP, WIDTH),
        out_grad,
    )


def solution(mesh):
    return jax.shard_map(
        on_device,
        mesh=mesh,
        in_specs=(P("ctx", None), P("ctx", None), P("ctx", None), P("ctx", None), P()),
        out_specs=(P("ctx", "dp"), P("ctx", "dp"), P(("dp", "ctx"), None), P(("dp", "ctx"), None)),
        check_vma=False,
    )
```

time: 1620 us -> 68.9 us (0.04)
  the two profiles are of different devices: /device:TPU:1 before, /device:TPU:0 now
where the time goes in v2:
time: 68.9 us; the launch traced here: 68.6 us
  Pallas kernels  64.3 us (93%)
  local copies, waits for them, and re-layouts  3.65 us (5%)
    pallas_call x1, Pallas kernels, on_device(): pl.pallas_call(kernel, out_shape=(tokens, tokens, terms, terms), in_specs...  64.3 us
    unnamed x10, local copies, waits for them, and re-layouts  3.65 us

profile of v2, /device:TPU:0, one launch (start us, length us, event | category | flops | bytes accessed | tf_op | source)
XLA Modules:
  0.0 68.6 jit_solution(13427485185664874895)
XLA Ops:
  0.6 64.3 %shard_map.84 = (bf16[256,256]{1,0:T(8,128)(2,1)}, bf16[256,256]{1,0:T(8,128)(2,1)}, bf16[64,128]{1,0:T(8,128)(2,1)}, bf16[64,128]{1,0:T(8,128)(2,1)}) custom-call(s32[64,128]{1,0:T(8,128)} %bitcast.5, bf16[256,1024]{1,0:T(8,128)(2,1)} %q_hbm.1, bf16[2,2,64,128]{3,2,1,0:T(8,128)(2,1)} %bitcast.3, bf16[2,2,64,128]{3,2,1,0:T(8,128)(2,1)} %bitcast.4, ...), custom_call_target="tpu_custom_call" | custom-call | tf_op jit(solution)/shard_map/pallas_call | solution.py:473
  65.0 0.0 copy-start
  65.0 1.6 %copy.13 = bf16[256,256]{1,0:T(8,128)(2,1)} copy(bf16[256,256]{1,0:T(8,128)(2,1)} %get-tuple-element.8) | data formatting | bytes 262144
  66.6 0.0 copy-done
  66.6 0.0 copy-start.2
  66.6 0.7 copy.14
  67.2 0.1 copy-done.2
  67.3 0.0 copy-start.1
  67.3 0.6 copy.15
  67.9 0.1 copy-done.1
  68.0 0.6 copy.16
Async XLA Ops:
  65.0 1.6 %copy-start = (bf16[256,256]{1,0:T(8,128)(2,1)S(1)}, bf16[256,256]{1,0:T(8,128)(2,1)}, u32[]{:S(2)}) copy-start(bf16[256,256]{1,0:T(8,128)(2,1)} %get-tuple-element.9) | copy-start | bytes 393220
  66.6 0.7 %copy-start.2 = (bf16[64,128]{1,0:T(8,128)(2,1)S(1)}, bf16[64,128]{1,0:T(8,128)(2,1)}, u32[]{:S(2)}) copy-start(bf16[64,128]{1,0:T(8,128)(2,1)} %get-tuple-element.10) | copy-start | bytes 49156
  67.3 0.7 %copy-start.1 = (bf16[64,128]{1,0:T(8,128)(2,1)S(1)}, bf16[64,128]{1,0:T(8,128)(2,1)}, u32[]{:S(2)}) copy-start(bf16[64,128]{1,0:T(8,128)(2,1)} %get-tuple-element.11) | copy-start | bytes 49156

commit v3 on v0

v3 whole, which is shorter than its diff:
```python
import math

import jax
import jax.numpy as jnp
from jax import lax
from jax.experimental import pallas as pl
from jax.experimental.pallas import tpu as pltpu
from jax.sharding import PartitionSpec as P

F32 = jnp.float32
BF16 = jnp.bfloat16
MESH = pl.DeviceIdType.MESH

N = 4
CHIPS = N * N
ROWS = 256
PAIR = 2 * ROWS
WIDTH = 128
SEQ = PAIR * CHIPS
GROUP = 128
HOME = 64
PER = 2
TILE = PER * GROUP
TILES = 9
HEADS = 2
DEVS = 4
NEG = -1e30


def dot(a, b):
    return lax.dot_general(a, b, (((1,), (0,)), ((), ())), preferred_element_type=F32)


def kernel(
    seg_hbm, q_hbm, k_hbm, v_hbm, g_hbm,
    out_hbm, dq_hbm, dk_hbm, dv_hbm,
    seg_ref, kall, vall, qbuf, gbuf, s_buf, e_buf,
    qa, gt, gpa, gp, mx, tot, o_t, dq_t, core_x, xs, xr, st, rng, dkv,
    part, rs, acc, final, obuf, orecv,
    load_sem, kv_sem, ag_send, ag_recv, pair_send, pair_recv, own_send, own_recv, x_send, x_recv, rel_send, rel_recv,
    st_send, st_recv, core_send, core_recv, sum_send, sum_recv, out_send, out_recv, rs_send, rs_recv, store_sem,
):
    p = lax.axis_index("dp")
    c = lax.axis_index("ctx")
    core = c % 2
    chip = c // 2
    z = chip % N
    y = chip // N
    xp = p % 2
    me = 2 * xp + core
    neighbour = p + 1 - 2 * xp
    sibling = (p, 2 * chip + 1 - core)
    partner = (p, 2 * (CHIPS - 1 - chip) + core)
    upper = (chip >= CHIPS // 2).astype(jnp.int32)
    own = 1 - upper
    lo = jnp.minimum(chip, CHIPS - 1 - chip)
    hi = CHIPS - 1 - lo
    n_hi = hi // PER + 1
    n_lo = lo // PER + 1
    n_own = jnp.where(upper == 1, n_hi, n_lo)
    n_other = TILES - n_own

    def beside(core_):
        return (neighbour, 2 * chip + core_)

    def head_of(slot, parity):
        return 2 * (p - xp + slot) + parity

    def plane_chip(n):
        there = ((y + n // N) % N) * N + (z + n % N) % N
        return there, jnp.maximum(there, CHIPS - 1 - there)

    def cols(head):
        return pl.ds(pl.multiple_of(head * WIDTH, WIDTH), WIDTH)

    home_z = 2 * core + xp
    src_x, src_core = z % 2, z // 2
    keeps = home_z == z
    mine = N * p + y

    def is_me(dev):
        return (dev[0] == p) & (dev[1] == c)

    def home_of(block, half):
        return (block // N, ((block % N) * N + home_z) * 2 + half)

    def source(n):
        return (src_x + 2 * (n // CHIPS), 2 * (n % CHIPS) + src_core)

    barrier = pltpu.get_barrier_semaphore()

    def greet(there):
        pl.semaphore_signal(barrier, inc=1, device_id=there, device_id_type=MESH)

    def greet_plane(n, carry):
        greet((p, 2 * plane_chip(n)[0] + core))
        return carry

    def greet_source(n, carry):
        there = source(n)

        @pl.when(jnp.logical_not(is_me(there)))
        def _():
            greet(there)

        return carry

    lax.fori_loop(1, CHIPS, greet_plane, 0)
    greet(beside(core))
    greet(beside(1 - core))
    greet(sibling)
    lax.fori_loop(0, 2 * CHIPS, greet_source, 0)

    kv_loads = [
        pltpu.make_async_copy(src.at[pl.ds(pl.multiple_of(GROUP * xp, GROUP), GROUP)], dst.at[chip], kv_sem.at[i])
        for i, (src, dst) in enumerate(((k_hbm, kall), (v_hbm, vall)))
    ]
    arrays = ((q_hbm, qbuf), (g_hbm, gbuf))
    loads = [
        pltpu.make_async_copy(src.at[:, cols(head_of(i, upper))], buf.at[own, i, core], load_sem.at[a, i])
        for a, (src, buf) in enumerate(arrays)
        for i in range(HEADS)
    ]
    seg_load = pltpu.make_async_copy(seg_hbm, seg_ref, kv_sem.at[2])
    for copy in kv_loads + loads + [seg_load]:
        copy.start()
    started = []

    def remote(src, dst, send, recv, there):
        return pltpu.make_async_remote_copy(
            src_ref=src, dst_ref=dst, send_sem=send, recv_sem=recv, device_id=there, device_id_type=MESH
        )

    def go(copy):
        copy.start()
        started.append(copy)
        return copy

    def block_copy(which, n):
        there, need = plane_chip(n)
        spot = (kall, vall)[which].at[chip]
        copy = remote(spot, spot, ag_send.at[which, n], ag_recv.at[which, chip], (p, 2 * there + core))
        return copy, need >= chip

    def each_block(which, act):
        def one(n, carry):
            copy, needed = block_copy(which, n)
            pl.when(needed)(lambda: act(copy))
            return carry

        lax.fori_loop(1, CHIPS, one, 0)

    def arrived(which, j):
        @pl.when((j != chip) & (j <= hi))
        def _():
            spot = (kall, vall)[which].at[j]
            remote(spot, spot, ag_send.at[which, 0], ag_recv.at[which, j], sibling).wait_recv()

    def pair_copy(a):
        src, buf = arrays[a]
        src = src.at[:, cols(2 * p + 1 - upper)]
        return remote(src, buf.at[own, xp, core], pair_send.at[a], pair_recv.at[a], partner)

    def share_own(a):
        spot = arrays[a][1].at[own, :, core]
        for i in range(HEADS):
            loads[HEADS * a + i].wait()
        go(remote(spot, spot, own_send.at[a], own_recv.at[a], sibling))

    def to_sibling(a, slot):
        spot = arrays[a][1].at[1 - own, slot, core]
        go(remote(spot, spot, rel_send.at[a, slot], rel_recv.at[a, slot], sibling))

    def share_pair(a):
        spot = arrays[a][1].at[1 - own, xp, core]
        remote(spot, spot, pair_send.at[a], pair_recv.at[a], partner).wait_recv()
        go(remote(spot, spot, x_send.at[a], x_recv.at[a], beside(core)))
        to_sibling(a, xp)

    def pass_on(a):
        spot = arrays[a][1].at[1 - own, 1 - xp, core]
        remote(spot, spot, x_send.at[a], x_recv.at[a], sibling).wait_recv()
        to_sibling(a, 1 - xp)

    def from_sibling(a):
        for i in range(HEADS):
            spot = arrays[a][1].at[1 - own, i, 1 - core]
            remote(spot, spot, rel_send.at[a, 0], rel_recv.at[a, i], sibling).wait_recv()

    def own_from_sibling(a):
        spot = arrays[a][1].at[own, :, 1 - core]
        remote(spot, spot, own_send.at[a], own_recv.at[a], sibling).wait_recv()

    pl.semaphore_wait(barrier, CHIPS - 1 + 2 + 1 + 2 * CHIPS - keeps.astype(jnp.int32))
    go(pair_copy(0))
    kv_loads[0].wait()
    each_block(0, lambda copy: copy.start())
    share_own(0)
    go(pair_copy(1))
    kv_loads[1].wait()
    each_block(1, lambda copy: copy.start())
    share_own(1)

    scale = WIDTH**-0.5
    seg_load.wait()
    seg = seg_ref[...]
    starts = [jnp.sum((seg < doc).astype(jnp.int32), axis=(0, 1), keepdims=True) for doc in (1, 2, 3)]
    lane = lax.broadcasted_iota(jnp.int32, (1, WIDTH), 1)
    for g, block in ((0, hi), (1, lo)):
        for i in range(PAIR // WIDTH):
            ids = seg_ref[pl.ds(block * (PAIR // WIDTH) + i, 1), :]
            start = jnp.where(
                ids == 0, 0, jnp.where(ids == 1, starts[0], jnp.where(ids == 2, starts[1], starts[2]))
            )
            rng[g, 0, :, i * WIDTH : (i + 1) * WIDTH] = start
            rng[g, 1, :, i * WIDTH : (i + 1) * WIDTH] = block * PAIR + i * WIDTH + lane
    mx[...] = jnp.full_like(mx, NEG)
    tot[...] = jnp.zeros_like(tot)

    def clear(i, carry):
        for ref in (o_t, dq_t):
            ref[i] = jnp.zeros_like(ref[i])
        return carry

    lax.fori_loop(0, HEADS, clear, 0)

    def clear_block(j, carry):
        for which in (0, 1):
            dkv[which, j] = jnp.zeros((GROUP, WIDTH), F32)
        return carry

    lax.fori_loop(0, CHIPS, clear_block, 0)

    def unused_block(j, carry):
        for ref in (kall, vall):
            ref[j] = jnp.zeros((GROUP, WIDTH), BF16)
        return carry

    lax.fori_loop(hi + 1, CHIPS, unused_block, 0)

    def scale_rows(g):
        def one(i, carry):
            for r in (0, 1):
                at = slice(r * ROWS, (r + 1) * ROWS)
                scaled = qbuf[g, i, r].astype(F32).T * (scale * math.log2(math.e))
                high = scaled.astype(BF16)
                qa[g, i, :WIDTH, at] = high
                qa[g, i, WIDTH:, at] = (scaled - high.astype(F32)).astype(BF16)
            return carry

        lax.fori_loop(0, HEADS, one, 0)

    def turn_grads(g):
        def one(i, carry):
            for r in (0, 1):
                gt[g, i, :, r * ROWS : (r + 1) * ROWS] = gbuf[g, i, r].T
            return carry

        lax.fori_loop(0, HEADS, one, 0)

    row = lax.broadcasted_iota(jnp.int32, (TILE, PAIR), 0)
    token = PAIR * (row // GROUP) + row % GROUP + ROWS * core + GROUP * xp

    def tile_of(ref, b):
        return ref[pl.ds(PER * b, PER)].reshape(TILE, WIDTH)

    def fold(op, values):
        return op(values.reshape(TILE // 8, 8, PAIR), axis=0)

    def scores_step(g, b):
        k = tile_of(kall, b)
        k = jnp.concatenate([k, k], axis=1)
        key = token + b * (PER * PAIR)
        seen = (key >= rng[g, 0]) & (key <= rng[g, 1])

        def one(i, carry):
            s = jnp.where(seen, dot(k, qa[g, i]), NEG)
            s_buf[i, b + g * n_hi] = s
            mx[i, g] = jnp.maximum(mx[i, g], fold(jnp.max, s))
            return carry

        lax.fori_loop(0, HEADS, one, 0)

    share_pair(0)
    own_from_sibling(0)
    scale_rows(own)

    def scores_own(b, carry):
        for j in range(PER):
            arrived(0, PER * b + j)

        @pl.when(b < n_own)
        def _():
            scores_step(own, b)

        return carry

    lax.fori_loop(0, n_hi, scores_own, 0)
    share_pair(1)
    pass_on(0)
    own_from_sibling(1)
    turn_grads(own)
    from_sibling(0)
    scale_rows(1 - own)

    def scores_other(b, carry):
        scores_step(1 - own, b)
        return carry

    lax.fori_loop(0, n_other, scores_other, 0)
    pass_on(1)
    lax.fori_loop(0, CHIPS, lambda j, carry: (arrived(1, j), carry)[1], 0)

    def over_tiles(step):
        def one(t, carry):
            g = (t >= n_hi).astype(jnp.int32)
            step(t, g, t - g * n_hi)
            return carry

        lax.fori_loop(0, TILES, one, 0)

    def statistics(i):
        for g in (0, 1):
            at = 4 * g
            st[i, me, at : at + 1] = mx[i, g, 0:1]
            st[i, me, at + 1 : at + 2] = jnp.sum(tot[i, g], axis=0, keepdims=True)
            o = jnp.concatenate([o_t[i, g, 0], o_t[i, g, 1]], axis=1)
            st[i, me, at + 2 : at + 3] = jnp.sum(gt[g, i].astype(F32) * o, axis=0, keepdims=True)
            st[i, me, at + 3 : at + 4] = jnp.zeros((1, PAIR), F32)
        spot = st.at[i, me]
        for slot, there in enumerate((beside(core), beside(1 - core), sibling)):
            go(remote(spot, spot, st_send.at[i, slot], st_recv.at[i, me], there))

    for n, i in enumerate((xp, 1 - xp)):
        for g in (0, 1):
            mx[i, g] = jnp.broadcast_to(jnp.max(mx[i, g], axis=0, keepdims=True), (8, PAIR))

        def weights_step(t, g, b, i=i):
            e = jnp.exp2(s_buf[i, t] - mx[i, g, 0:1])
            tot[i, g] = tot[i, g] + fold(jnp.sum, e)
            e = e.astype(BF16)
            e_buf[i, t] = e
            o = dot(tile_of(vall, b).T, e)
            for r in (0, 1):
                o_t[i, g, r] = o_t[i, g, r] + o[:, r * ROWS : (r + 1) * ROWS]

        over_tiles(weights_step)
        if n == 0:
            from_sibling(1)
            turn_grads(1 - own)
        statistics(i)

    ones = jnp.ones((TILE, WIDTH), BF16)
    sub = lax.broadcasted_iota(jnp.int32, (WIDTH, PAIR), 0)

    def prepare(i):
        for other in (2 * (1 - xp), 2 * (1 - xp) + 1, 2 * xp + 1 - core):
            spot = st.at[i, other]
            remote(spot, spot, st_send.at[i, 0], st_recv.at[i, other], sibling).wait_recv()
        for g in (0, 1):
            at = 4 * g
            tops = [st[i, s, at : at + 1] for s in range(DEVS)]
            top = jnp.maximum(jnp.maximum(tops[0], tops[1]), jnp.maximum(tops[2], tops[3]))
            total = delta = jnp.zeros((1, PAIR), F32)
            for s in range(DEVS):
                by = jnp.exp2(tops[s] - top)
                total = total + by * st[i, s, at + 1 : at + 2]
                delta = delta + by * st[i, s, at + 2 : at + 3]
            inv = 1.0 / total
            factor = jnp.exp2(st[i, me, at : at + 1] - top) * inv
            delta = -delta * inv * factor
            for r in (0, 1):
                o_t[i, g, r] = o_t[i, g, r] * factor[:, r * ROWS : (r + 1) * ROWS]
            grad = (gt[g, i].astype(F32) * factor).astype(BF16)
            gpa[i, g, :WIDTH] = grad
            gp[i, g] = grad.T
            d1 = delta.astype(BF16).astype(F32)
            d2 = (delta - d1).astype(BF16).astype(F32)
            extra = jnp.where(sub == 0, d1, jnp.where(sub == 1, d2, jnp.where(sub == 2, delta - d1 - d2, 0.0)))
            gpa[i, g, WIDTH:] = extra.astype(BF16)

    parts_of = (o_t, dq_t)

    def to_core(kind, i, g):
        go(
            remote(
                parts_of[kind].at[i, g, 1 - core], core_x.at[kind, i, g],
                core_send.at[kind, i, g], core_recv.at[kind, i, g], sibling,
            )
        )

    def from_core(kind, i, g):
        spot = core_x.at[kind, i, g]
        remote(spot, spot, core_send.at[kind, i, g], core_recv.at[kind, i, g], sibling).wait_recv()
        return parts_of[kind][i, g, core] + core_x[kind, i, g]

    def to_beside(kind, g):
        xs[kind, g] = from_core(kind, 1 - xp, g).astype(BF16)
        go(remote(xs.at[kind, g], xr.at[kind, g], sum_send.at[kind, g], sum_recv.at[kind, g], beside(core)))

    stores = []

    def store(src, dst, i):
        stores.append(pltpu.make_async_copy(src, dst, store_sem.at[i]))
        stores[-1].start()

    def finish(kind, g):
        total = from_core(kind, xp, g)
        spot = xr.at[kind, g]
        remote(spot, spot, sum_send.at[kind, g], sum_recv.at[kind, g], sibling).wait_recv()
        total = total + xr[kind, g].astype(F32)
        if kind == 1:
            total = total * scale
        obuf[kind, g] = total.T.astype(BF16)

    def finish_own(kind):
        finish(kind, own)
        store(obuf.at[kind, own], (out_hbm, dq_hbm)[kind].at[:, cols(upper)], kind)

    def partner_copy(kind):
        return remote(obuf.at[kind, 1 - own], orecv.at[kind], out_send.at[kind], out_recv.at[kind], partner)

    def finish_other(kind):
        finish(kind, 1 - own)
        go(partner_copy(kind))

    def from_partner(kind):
        partner_copy(kind).wait_recv()
        store(orecv.at[kind], (out_hbm, dq_hbm)[kind].at[:, cols(1 - upper)], 2 + kind)

    def grad_copy(block, half):
        there = home_of(block, half)
        copy = remote(
            part.at[block, half], rs.at[me_source], rs_send.at[block, half], rs_recv.at[me_source], there
        )
        return copy, (block <= hi) & jnp.logical_not(is_me(there))

    me_source = (p // 2) * CHIPS + chip

    def each_half(block, act):
        for half in (0, 1):
            copy, needed = grad_copy(block, half)
            pl.when(needed)(lambda copy=copy: act(copy))

    def send_grads(b):
        for block in (PER * b, PER * b + 1):
            for half in (0, 1):
                at = slice(half * HOME, (half + 1) * HOME)
                part[block, half, 0] = (dkv[0, block, at] * scale).astype(BF16)
                part[block, half, 1] = dkv[1, block, at].astype(BF16)
            each_half(block, lambda copy: copy.start())

    def grads_pass(g, i, leave):
        n_tiles = jnp.where(g == 0, n_hi, n_lo)
        turn = (2 * p + y + 2 * z) % n_tiles

        def one(n, carry):
            b = (n + turn) % n_tiles
            e = e_buf[i, b + g * n_hi]
            k = tile_of(kall, b)
            dp = dot(jnp.concatenate([tile_of(vall, b), ones], axis=1), gpa[i, g])
            ds = (e.astype(F32) * dp).astype(BF16)
            at = pl.ds(PER * b, PER)
            dkv[0, at] = dkv[0, at] + dot(ds, qbuf[g, i].reshape(PAIR, WIDTH)).reshape(PER, GROUP, WIDTH)
            dkv[1, at] = dkv[1, at] + dot(e, gp[i, g]).reshape(PER, GROUP, WIDTH)
            dq = dot(k.T, ds)
            for r in (0, 1):
                dq_t[i, g, r] = dq_t[i, g, r] + dq[:, r * ROWS : (r + 1) * ROWS]
            if leave is not None:
                pl.when(leave(b))(lambda: send_grads(b))
            return carry

        lax.fori_loop(0, n_tiles, one, 0)
        to_core(1, i, g)

    prepare(1 - xp)
    for g in (0, 1):
        to_core(0, 1 - xp, g)
    grads_pass(1 - own, 1 - xp, None)
    prepare(xp)
    for g in (0, 1):
        to_core(0, xp, g)
    for g in (0, 1):
        to_beside(0, g)
    grads_pass(1 - own, xp, lambda b: b >= n_own)
    to_beside(1, 1 - own)
    finish_other(0)
    grads_pass(own, 1 - xp, None)
    finish_other(1)
    finish_own(0)
    grads_pass(own, xp, lambda b: b < n_own)
    to_beside(1, own)

    mine_half = core
    acc[...] = jnp.where(keeps & (mine <= hi), part[mine, mine_half].astype(F32), 0.0)

    def add_source(n, carry):
        slot = (me_source + n) % (2 * CHIPS)
        k = slot % CHIPS
        sends = jnp.maximum(k, CHIPS - 1 - k) >= mine

        @pl.when(sends & jnp.logical_not(is_me(source(slot))))
        def _():
            spot = rs.at[slot]
            remote(spot, spot, rs_send.at[0, 0], rs_recv.at[slot], sibling).wait_recv()
            acc[...] = acc[...] + rs[slot].astype(F32)

        return carry

    from_partner(0)
    finish_own(1)
    lax.fori_loop(0, 2 * CHIPS, add_source, 0)
    final[...] = acc[...].astype(BF16)
    store(final.at[0], dk_hbm, 4)
    store(final.at[1], dv_hbm, 5)
    from_partner(1)
    for which in (0, 1):
        each_block(which, lambda copy: copy.wait_send())

    def sent(block, carry):
        each_half(block, lambda copy: copy.wait_send())
        return carry

    lax.fori_loop(0, CHIPS, sent, 0)
    for copy in started:
        copy.wait_send()
    for copy in stores:
        copy.wait()


def on_device(queries, keys, values, out_grad, segment_ids):
    hbm = pl.BlockSpec(memory_space=pl.ANY)
    dma = pltpu.SemaphoreType.DMA
    vmem = pltpu.VMEM
    scratch = [
        vmem((SEQ // WIDTH, WIDTH), jnp.int32),
        vmem((CHIPS, GROUP, WIDTH), BF16),
        vmem((CHIPS, GROUP, WIDTH), BF16),
        vmem((2, HEADS, 2, ROWS, WIDTH), BF16),
        vmem((2, HEADS, 2, ROWS, WIDTH), BF16),
        vmem((HEADS, TILES, TILE, PAIR), F32),
        vmem((HEADS, TILES, TILE, PAIR), BF16),
        vmem((2, HEADS, 2 * WIDTH, PAIR), BF16),
        vmem((2, HEADS, WIDTH, PAIR), BF16),
        vmem((HEADS, 2, 2 * WIDTH, PAIR), BF16),
        vmem((HEADS, 2, PAIR, WIDTH), BF16),
        vmem((HEADS, 2, 8, PAIR), F32),
        vmem((HEADS, 2, 8, PAIR), F32),
        vmem((HEADS, 2, 2, WIDTH, ROWS), F32),
        vmem((HEADS, 2, 2, WIDTH, ROWS), F32),
        vmem((2, HEADS, 2, WIDTH, ROWS), F32),
        vmem((2, 2, WIDTH, ROWS), BF16),
        vmem((2, 2, WIDTH, ROWS), BF16),
        vmem((HEADS, DEVS, 8, PAIR), F32),
        vmem((2, 2, 1, PAIR), jnp.int32),
        vmem((2, CHIPS, GROUP, WIDTH), F32),
        vmem((CHIPS, 2, 2, HOME, WIDTH), BF16),
        vmem((2 * CHIPS, 2, HOME, WIDTH), BF16),
        vmem((2, HOME, WIDTH), F32),
        vmem((2, HOME, WIDTH), BF16),
        vmem((2, 2, ROWS, WIDTH), BF16),
        vmem((2, ROWS, WIDTH), BF16),
        dma((2, HEADS)),
        dma((3,)),
        dma((2, CHIPS)), dma((2, CHIPS)),
        dma((2,)), dma((2,)),
        dma((2,)), dma((2,)),
        dma((2,)), dma((2,)),
        dma((2, HEADS)), dma((2, HEADS)),
        dma((HEADS, 3)), dma((HEADS, DEVS)),
        dma((2, HEADS, 2)), dma((2, HEADS, 2)),
        dma((2, 2)), dma((2, 2)),
        dma((2,)), dma((2,)),
        dma((CHIPS, 2)), dma((2 * CHIPS,)),
        dma((6,)),
    ]
    tokens = jax.ShapeDtypeStruct((ROWS, 2 * WIDTH), BF16)
    terms = jax.ShapeDtypeStruct((HOME, WIDTH), BF16)
    return pl.pallas_call(
        kernel,
        out_shape=(tokens, tokens, terms, terms),
        in_specs=[hbm] * 5,
        out_specs=(hbm,) * 4,
        scratch_shapes=scratch,
        compiler_params=pltpu.CompilerParams(
            collective_id=0, has_side_effects=True, vmem_limit_bytes=56 * 1024 * 1024
        ),
    )(segment_ids.reshape(SEQ // WIDTH, WIDTH), queries, keys, values, out_grad)


def solution(mesh):
    return jax.shard_map(
        on_device,
        mesh=mesh,
        in_specs=(P("ctx", None), P("ctx", None), P("ctx", None), P("ctx", None), P()),
        out_specs=(P("ctx", "dp"), P("ctx", "dp"), P(("dp", "ctx"), None), P(("dp", "ctx"), None)),
        check_vma=False,
    )
```

time: 1620 us -> 75.2 us (0.05)
  the two profiles are of different devices: /device:TPU:1 before, /device:TPU:25 now
where the time goes in v3:
time: 75.2 us; the launch traced here: 74.9 us
  Pallas kernels  70.6 us (94%)
  local copies, waits for them, and re-layouts  3.65 us (5%)
    pallas_call x1, Pallas kernels, on_device(): pl.pallas_call(kernel, out_shape=(tokens, tokens, terms, terms), in_specs...  70.6 us
    unnamed x10, local copies, waits for them, and re-layouts  3.65 us

profile of v3, /device:TPU:25, one launch (start us, length us, event | category | flops | bytes accessed | tf_op | source)
XLA Modules:
  0.0 74.9 jit_solution(16036869658535882803)
XLA Ops:
  0.6 70.6 %shard_map.84 = (bf16[256,256]{1,0:T(8,128)(2,1)}, bf16[256,256]{1,0:T(8,128)(2,1)}, bf16[64,128]{1,0:T(8,128)(2,1)}, bf16[64,128]{1,0:T(8,128)(2,1)}) custom-call(s32[64,128]{1,0:T(8,128)} %bitcast.1, bf16[256,1024]{1,0:T(8,128)(2,1)} %q_hbm.1, bf16[256,128]{1,0:T(8,128)(2,1)} %k_hbm.1, bf16[256,128]{1,0:T(8,128)(2,1)} %v_hbm.1, bf16[256,1024]{1,0:T(8,128)(2,1)} %g_hbm.1), custom_call_target="tpu_custom_call" | custom-call | tf_op jit(solution)/shard_map/pallas_call | solution.py:579
  71.2 0.0 copy-start
  71.3 1.6 %copy.13 = bf16[256,256]{1,0:T(8,128)(2,1)} copy(bf16[256,256]{1,0:T(8,128)(2,1)} %get-tuple-element.8) | data formatting | bytes 262144
  72.9 0.0 copy-done
  72.9 0.0 copy-start.2
  72.9 0.7 copy.14
  73.5 0.1 copy-done.2
  73.6 0.0 copy-start.1
  73.6 0.6 copy.15
  74.2 0.1 copy-done.1
  74.3 0.6 copy.16
Async XLA Ops:
  71.2 1.6 %copy-start = (bf16[256,256]{1,0:T(8,128)(2,1)S(1)}, bf16[256,256]{1,0:T(8,128)(2,1)}, u32[]{:S(2)}) copy-start(bf16[256,256]{1,0:T(8,128)(2,1)} %get-tuple-element.9) | copy-start | bytes 393220
  72.9 0.7 copy-start.2
  73.6 0.7 copy-start.1

commit v4 on v3

--- a/solution.py
+++ b/solution.py
@@ -36,9 +36,9 @@
     out_hbm, dq_hbm, dk_hbm, dv_hbm,
     seg_ref, kall, vall, qbuf, gbuf, s_buf, e_buf,
     qa, gt, gpa, gp, mx, tot, o_t, dq_t, core_x, xs, xr, st, rng, dkv,
-    part, rs, acc, final, obuf, orecv,
+    part, r1, d2, r2, d3, r3, acc, sums, final, obuf, orecv,
     load_sem, kv_sem, ag_send, ag_recv, pair_send, pair_recv, own_send, own_recv, x_send, x_recv, rel_send, rel_recv,
-    st_send, st_recv, core_send, core_recv, sum_send, sum_recv, out_send, out_recv, rs_send, rs_recv, store_sem,
+    st_send, st_recv, core_send, core_recv, sum_send, sum_recv, out_send, out_recv, r1_send, r1_recv, r2_send, r2_recv, r3_send, r3_recv, store_sem,
 ):
     p = lax.axis_index("dp")
     c = lax.axis_index("ctx")
@@ -66,53 +66,48 @@
     def head_of(slot, parity):
         return 2 * (p - xp + slot) + parity
 
-    def plane_chip(n):
-        there = ((y + n // N) % N) * N + (z + n % N) % N
-        return there, jnp.maximum(there, CHIPS - 1 - there)
+    def along(axis, d):
+        there = dict(y=y, z=z)
+        there[axis] = (there[axis] + d) % N
+        return (p, (there["y"] * N + there["z"]) * 2 + core)
+
+    def chip_at(dy, dz):
+        return ((y + N - dy) % N) * N + (z + N - dz) % N
+
+    def upper_of(k):
+        return jnp.maximum(k, CHIPS - 1 - k)
 
     def cols(head):
         return pl.ds(pl.multiple_of(head * WIDTH, WIDTH), WIDTH)
 
     home_z = 2 * core + xp
-    src_x, src_core = z % 2, z // 2
-    keeps = home_z == z
-    mine = N * p + y
+
+    def home(half):
+        return (z, (y * N + home_z) * 2 + half)
+
+    def source(u):
+        return (z % 2 + 2 * u, (y * N + p) * 2 + z // 2)
 
     def is_me(dev):
         return (dev[0] == p) & (dev[1] == c)
 
-    def home_of(block, half):
-        return (block // N, ((block % N) * N + home_z) * 2 + half)
-
-    def source(n):
-        return (src_x + 2 * (n // CHIPS), 2 * (n % CHIPS) + src_core)
+    keeps = (z == p) & (home_z == z)
 
     barrier = pltpu.get_barrier_semaphore()
 
     def greet(there):
         pl.semaphore_signal(barrier, inc=1, device_id=there, device_id_type=MESH)
 
-    def greet_plane(n, carry):
-        greet((p, 2 * plane_chip(n)[0] + core))
-        return carry
-
-    def greet_source(n, carry):
-        there = source(n)
-
-        @pl.when(jnp.logical_not(is_me(there)))
-        def _():
-            greet(there)
-
-        return carry
-
-    lax.fori_loop(1, CHIPS, greet_plane, 0)
-    greet(beside(core))
-    greet(beside(1 - core))
-    greet(sibling)
-    lax.fori_loop(0, 2 * CHIPS, greet_source, 0)
+    for d in range(1, N):
+        for axis in "yz":
+            greet(along(axis, d))
+    for there in (partner, beside(core), beside(1 - core), sibling):
+        greet(there)
+    for u in (0, 1):
+        pl.when(jnp.logical_not(is_me(source(u))))(lambda u=u: greet(source(u)))
 
     kv_loads = [
-        pltpu.make_async_copy(src.at[pl.ds(pl.multiple_of(GROUP * xp, GROUP), GROUP)], dst.at[chip], kv_sem.at[i])
+        pltpu.make_async_copy(src.at[xp], dst.at[chip], kv_sem.at[i])
         for i, (src, dst) in enumerate(((k_hbm, kall), (v_hbm, vall)))
     ]
     arrays = ((q_hbm, qbuf), (g_hbm, gbuf))
@@ -136,25 +131,46 @@
         started.append(copy)
         return copy
 
-    def block_copy(which, n):
-        there, need = plane_chip(n)
-        spot = (kall, vall)[which].at[chip]
-        copy = remote(spot, spot, ag_send.at[which, n], ag_recv.at[which, chip], (p, 2 * there + core))
-        return copy, need >= chip
-
-    def each_block(which, act):
-        def one(n, carry):
-            copy, needed = block_copy(which, n)
-            pl.when(needed)(lambda: act(copy))
-            return carry
-
-        lax.fori_loop(1, CHIPS, one, 0)
-
-    def arrived(which, j):
-        @pl.when((j != chip) & (j <= hi))
-        def _():
-            spot = (kall, vall)[which].at[j]
-            remote(spot, spot, ag_send.at[which, 0], ag_recv.at[which, j], sibling).wait_recv()
+    whole = (kall, vall)
+    count = [0, 0]
+    key_copies = []
+
+    def push(which, block, half, there):
+        spot = whole[which].at[block, half]
+        copy = remote(spot, spot, ag_send.at[which, count[which]], ag_recv.at[which, block, half], there)
+        count[which] += 1
+        if which == 0:
+            copy.start()
+            key_copies.append(copy)
+        else:
+            go(copy)
+
+    def arrived(which, block, half):
+        spot = whole[which].at[block, half]
+        remote(spot, spot, ag_send.at[which, 0], ag_recv.at[which, block, half], sibling).wait_recv()
+
+    def push_mine(which):
+        for axes in ("yz", "zy"):
+            for d in (1, 3, 2):
+                for half in (0, 1):
+                    push(which, chip, half, along(axes[half], d))
+
+    def relay(which):
+        for d in (1, 3, 2):
+            for half, block in ((0, chip_at(d, 0)), (1, chip_at(0, d))):
+                arrived(which, block, half)
+                for d2 in (1, 3, 2):
+                    push(which, block, half, along("zy"[half], d2))
+
+    def tile_in_order(n):
+        turn = n // 2
+        row_ = (y + jnp.where(turn == 2, 3, jnp.where(turn == 3, 2, turn))) % N
+        return 2 * row_ + n % 2
+
+    def tile_arrived(which, b):
+        for j in (PER * b, PER * b + 1):
+            pl.when(j % N != z)(lambda j=j: arrived(which, j, 0))
+            pl.when(j // N != y)(lambda j=j: arrived(which, j, 1))
 
     def pair_copy(a):
         src, buf = arrays[a]
@@ -191,15 +207,13 @@
         spot = arrays[a][1].at[own, :, 1 - core]
         remote(spot, spot, own_send.at[a], own_recv.at[a], sibling).wait_recv()
 
-    pl.semaphore_wait(barrier, CHIPS - 1 + 2 + 1 + 2 * CHIPS - keeps.astype(jnp.int32))
+    pl.semaphore_wait(barrier, 12 - keeps.astype(jnp.int32))
     go(pair_copy(0))
     kv_loads[0].wait()
-    each_block(0, lambda copy: copy.start())
+    push_mine(0)
     share_own(0)
     go(pair_copy(1))
-    kv_loads[1].wait()
-    each_block(1, lambda copy: copy.start())
-    share_own(1)
+    relay(0)
 
     scale = WIDTH**-0.5
     seg_load.wait()
@@ -231,13 +245,6 @@
 
     lax.fori_loop(0, CHIPS, clear_block, 0)
 
-    def unused_block(j, carry):
-        for ref in (kall, vall):
-            ref[j] = jnp.zeros((GROUP, WIDTH), BF16)
-        return carry
-
-    lax.fori_loop(hi + 1, CHIPS, unused_block, 0)
-
     def scale_rows(g):
         def one(i, carry):
             for r in (0, 1):
@@ -285,9 +292,9 @@
     own_from_sibling(0)
     scale_rows(own)
 
-    def scores_own(b, carry):
-        for j in range(PER):
-            arrived(0, PER * b + j)
+    def scores_own(n, carry):
+        b = tile_in_order(n)
+        tile_arrived(0, b)
 
         @pl.when(b < n_own)
         def _():
@@ -295,9 +302,16 @@
 
         return carry
 
-    lax.fori_loop(0, n_hi, scores_own, 0)
+    lax.fori_loop(0, 2, scores_own, 0)
+    for copy in key_copies:
+        copy.wait_send()
+    kv_loads[1].wait()
+    push_mine(1)
+    share_own(1)
+    pass_on(0)
+    lax.fori_loop(2, CHIPS // PER, scores_own, 0)
+    relay(1)
     share_pair(1)
-    pass_on(0)
     own_from_sibling(1)
     turn_grads(own)
     from_sibling(0)
@@ -309,7 +323,7 @@
 
     lax.fori_loop(0, n_other, scores_other, 0)
     pass_on(1)
-    lax.fori_loop(0, CHIPS, lambda j, carry: (arrived(1, j), carry)[1], 0)
+    lax.fori_loop(0, CHIPS // PER, lambda n, carry: (tile_arrived(1, tile_in_order(n)), carry)[1], 0)
 
     def over_tiles(step):
         def one(t, carry):
@@ -428,100 +442,147 @@
         partner_copy(kind).wait_recv()
         store(orecv.at[kind], (out_hbm, dq_hbm)[kind].at[:, cols(1 - upper)], 2 + kind)
 
-    def grad_copy(block, half):
-        there = home_of(block, half)
+    def touched(k, j):
+        return j // PER <= upper_of(k) // PER
+
+    def first_copy(which, j):
+        axis = "yz"[which]
+        d = (j % N + N - y) % N if which == 0 else (j // N + N - z) % N
+        index = j // N if which == 0 else j % N
         copy = remote(
-            part.at[block, half], rs.at[me_source], rs_send.at[block, half], rs_recv.at[me_source], there
+            part.at[which, j], r1.at[which, d - 1, index], r1_send.at[which, j], r1_recv.at[which, d - 1, index],
+            along(axis, d),
         )
-        return copy, (block <= hi) & jnp.logical_not(is_me(there))
-
-    me_source = (p // 2) * CHIPS + chip
-
-    def each_half(block, act):
-        for half in (0, 1):
-            copy, needed = grad_copy(block, half)
+        return copy, d != 0
+
+    def each_first(j, act):
+        for which in (0, 1):
+            copy, needed = first_copy(which, j)
             pl.when(needed)(lambda copy=copy: act(copy))
 
     def send_grads(b):
-        for block in (PER * b, PER * b + 1):
-            for half in (0, 1):
-                at = slice(half * HOME, (half + 1) * HOME)
-                part[block, half, 0] = (dkv[0, block, at] * scale).astype(BF16)
-                part[block, half, 1] = dkv[1, block, at].astype(BF16)
-            each_half(block, lambda copy: copy.start())
-
-    def grads_pass(g, i, leave):
-        n_tiles = jnp.where(g == 0, n_hi, n_lo)
-        turn = (2 * p + y + 2 * z) % n_tiles
-
+        for j in (PER * b, PER * b + 1):
+            part[0, j] = (dkv[0, j] * scale).astype(BF16)
+            part[1, j] = dkv[1, j].astype(BF16)
+            each_first(j, lambda copy: copy.start())
+
+    def grads_step(g, i, b):
+        e = e_buf[i, b + g * n_hi]
+        k = tile_of(kall, b)
+        dp = dot(jnp.concatenate([tile_of(vall, b), ones], axis=1), gpa[i, g])
+        ds = (e.astype(F32) * dp).astype(BF16)
+        at = pl.ds(PER * b, PER)
+        dkv[0, at] = dkv[0, at] + dot(ds, qbuf[g, i].reshape(PAIR, WIDTH)).reshape(PER, GROUP, WIDTH)
+        dkv[1, at] = dkv[1, at] + dot(e, gp[i, g]).reshape(PER, GROUP, WIDTH)
+        dq = dot(k.T, ds)
+        for r in (0, 1):
+            dq_t[i, g, r] = dq_t[i, g, r] + dq[:, r * ROWS : (r + 1) * ROWS]
+
+    def grads_pass(i, leave):
         def one(n, carry):
-            b = (n + turn) % n_tiles
-            e = e_buf[i, b + g * n_hi]
-            k = tile_of(kall, b)
-            dp = dot(jnp.concatenate([tile_of(vall, b), ones], axis=1), gpa[i, g])
-            ds = (e.astype(F32) * dp).astype(BF16)
-            at = pl.ds(PER * b, PER)
-            dkv[0, at] = dkv[0, at] + dot(ds, qbuf[g, i].reshape(PAIR, WIDTH)).reshape(PER, GROUP, WIDTH)
-            dkv[1, at] = dkv[1, at] + dot(e, gp[i, g]).reshape(PER, GROUP, WIDTH)
-            dq = dot(k.T, ds)
-            for r in (0, 1):
-                dq_t[i, g, r] = dq_t[i, g, r] + dq[:, r * ROWS : (r + 1) * ROWS]
-            if leave is not None:
-                pl.when(leave(b))(lambda: send_grads(b))
+            b = (2 * z + 2 + n) % (CHIPS // PER)
+            pl.when(b < n_hi)(lambda: grads_step(0, i, b))
+            pl.when(b < n_lo)(lambda: grads_step(1, i, b))
+            if leave:
+                pl.when(b < n_hi)(lambda: send_grads(b))
             return carry
 
-        lax.fori_loop(0, n_tiles, one, 0)
-        to_core(1, i, g)
+        lax.fori_loop(0, CHIPS // PER, one, 0)
+        for g in (0, 1):
+            to_core(1, i, g)
 
     prepare(1 - xp)
     for g in (0, 1):
         to_core(0, 1 - xp, g)
-    grads_pass(1 - own, 1 - xp, None)
+    grads_pass(1 - xp, False)
     prepare(xp)
     for g in (0, 1):
         to_core(0, xp, g)
-    for g in (0, 1):
-        to_beside(0, g)
-    grads_pass(1 - own, xp, lambda b: b >= n_own)
-    to_beside(1, 1 - own)
+    for kind in (0, 1):
+        for g in (0, 1):
+            to_beside(kind, g)
+    grads_pass(xp, True)
+
+    def second_copy(which, i):
+        d = (i + N - (z if which == 0 else y)) % N
+        copy = remote(
+            d2.at[which, i], r2.at[which, d - 1], r2_send.at[which, i], r2_recv.at[which, d - 1],
+            along("zy"[which], d),
+        )
+        return copy, d != 0
+
+    def first_sum(i, carry):
+        for which in (0, 1):
+            j = N * i + y if which == 0 else N * z + i
+            acc[...] = jnp.where(touched(chip, j), part[which, j].astype(F32), 0.0)
+            for s in range(N - 1):
+                k = chip_at(s + 1, 0) if which == 0 else chip_at(0, s + 1)
+
+                @pl.when(touched(k, j))
+                def _(s=s):
+                    spot = r1.at[which, s, i]
+                    remote(spot, spot, r1_send.at[which, 0], r1_recv.at[which, s, i], sibling).wait_recv()
+                    acc[...] = acc[...] + r1[which, s, i].astype(F32)
+
+            d2[which, i] = acc[...].astype(BF16)
+            copy, needed = second_copy(which, i)
+            pl.when(needed)(lambda copy=copy: copy.start())
+        return carry
+
+    lax.fori_loop(0, N, first_sum, 0)
+    finish_other(1)
+    for which, i in ((0, z), (1, y)):
+        total = d2[which, i].astype(F32)
+        for s in range(N - 1):
+            spot = r2.at[which, s]
+            remote(spot, spot, r2_send.at[which, 0], r2_recv.at[which, s], sibling).wait_recv()
+            total = total + r2[which, s].astype(F32)
+        total = total.astype(BF16)
+        for half in (0, 1):
+            d3[half, which] = total[half * HOME : (half + 1) * HOME]
+
+    def third_copy(half):
+        there = home(half)
+        copy = remote(d3.at[half], r3.at[p // 2], r3_send.at[half], r3_recv.at[p // 2], there)
+        return copy, jnp.logical_not(is_me(there))
+
+    for half in (0, 1):
+        copy, needed = third_copy(half)
+        pl.when(needed)(lambda copy=copy: copy.start())
+    finish_own(1)
     finish_other(0)
-    grads_pass(own, 1 - xp, None)
-    finish_other(1)
     finish_own(0)
-    grads_pass(own, xp, lambda b: b < n_own)
-    to_beside(1, own)
-
-    mine_half = core
-    acc[...] = jnp.where(keeps & (mine <= hi), part[mine, mine_half].astype(F32), 0.0)
-
-    def add_source(n, carry):
-        slot = (me_source + n) % (2 * CHIPS)
-        k = slot % CHIPS
-        sends = jnp.maximum(k, CHIPS - 1 - k) >= mine
-
-        @pl.when(sends & jnp.logical_not(is_me(source(slot))))
-        def _():
-            spot = rs.at[slot]
-            remote(spot, spot, rs_send.at[0, 0], rs_recv.at[slot], sibling).wait_recv()
-            acc[...] = acc[...] + rs[slot].astype(F32)
-
-        return carry
-
-    from_partner(0)
-    finish_own(1)
-    lax.fori_loop(0, 2 * CHIPS, add_source, 0)
-    final[...] = acc[...].astype(BF16)
+    total = jnp.where(keeps, d3[core].astype(F32), 0.0)
+    sums[...] = total
+    for u in (0, 1):
+
+        @pl.when(jnp.logical_not(is_me(source(u))))
+        def _(u=u):
+            spot = r3.at[u]
+            remote(spot, spot, r3_send.at[0], r3_recv.at[u], sibling).wait_recv()
+            sums[...] = sums[...] + r3[u].astype(F32)
+
+    final[...] = sums[...].astype(BF16)
     store(final.at[0], dk_hbm, 4)
     store(final.at[1], dv_hbm, 5)
+    from_partner(0)
     from_partner(1)
+
+    def sent(j, carry):
+        @pl.when(j // PER < n_hi)
+        def _():
+            each_first(j, lambda copy: copy.wait_send())
+
+        return carry
+
+    lax.fori_loop(0, CHIPS, sent, 0)
     for which in (0, 1):
-        each_block(which, lambda copy: copy.wait_send())
-
-    def sent(block, carry):
-        each_half(block, lambda copy: copy.wait_send())
-        return carry
-
-    lax.fori_loop(0, CHIPS, sent, 0)
+        for i in range(N):
+            copy, needed = second_copy(which, i)
+            pl.when(needed)(lambda copy=copy: copy.wait_send())
+    for half in (0, 1):
+        copy, needed = third_copy(half)
+        pl.when(needed)(lambda copy=copy: copy.wait_send())
     for copy in started:
         copy.wait_send()
     for copy in stores:
@@ -534,8 +595,8 @@
     vmem = pltpu.VMEM
     scratch = [
         vmem((SEQ // WIDTH, WIDTH), jnp.int32),
-        vmem((CHIPS, GROUP, WIDTH), BF16),
-        vmem((CHIPS, GROUP, WIDTH), BF16),
+        vmem((CHIPS, 2, HOME, WIDTH), BF16),
+        vmem((CHIPS, 2, HOME, WIDTH), BF16),
         vmem((2, HEADS, 2, ROWS, WIDTH), BF16),
         vmem((2, HEADS, 2, ROWS, WIDTH), BF16),
         vmem((HEADS, TILES, TILE, PAIR), F32),
@@ -554,15 +615,20 @@
         vmem((HEADS, DEVS, 8, PAIR), F32),
         vmem((2, 2, 1, PAIR), jnp.int32),
         vmem((2, CHIPS, GROUP, WIDTH), F32),
-        vmem((CHIPS, 2, 2, HOME, WIDTH), BF16),
-        vmem((2 * CHIPS, 2, HOME, WIDTH), BF16),
+        vmem((2, CHIPS, GROUP, WIDTH), BF16),
+        vmem((2, N - 1, N, GROUP, WIDTH), BF16),
+        vmem((2, N, GROUP, WIDTH), BF16),
+        vmem((2, N - 1, GROUP, WIDTH), BF16),
+        vmem((2, 2, HOME, WIDTH), BF16),
+        vmem((2, 2, HOME, WIDTH), BF16),
+        vmem((GROUP, WIDTH), F32),
         vmem((2, HOME, WIDTH), F32),
         vmem((2, HOME, WIDTH), BF16),
         vmem((2, 2, ROWS, WIDTH), BF16),
         vmem((2, ROWS, WIDTH), BF16),
         dma((2, HEADS)),
         dma((3,)),
-        dma((2, CHIPS)), dma((2, CHIPS)),
+        dma((2, 32)), dma((2, CHIPS, 2)),
         dma((2,)), dma((2,)),
         dma((2,)), dma((2,)),
         dma((2,)), dma((2,)),
@@ -571,7 +637,9 @@
         dma((2, HEADS, 2)), dma((2, HEADS, 2)),
         dma((2, 2)), dma((2, 2)),
         dma((2,)), dma((2,)),
-        dma((CHIPS, 2)), dma((2 * CHIPS,)),
+        dma((2, CHIPS)), dma((2, N - 1, N)),
+        dma((2, N)), dma((2, N - 1)),
+        dma((2,)), dma((2,)),
         dma((6,)),
     ]
     tokens = jax.ShapeDtypeStruct((ROWS, 2 * WIDTH), BF16)
@@ -585,7 +653,13 @@
         compiler_params=pltpu.CompilerParams(
             collective_id=0, has_side_effects=True, vmem_limit_bytes=56 * 1024 * 1024
         ),
-    )(segment_ids.reshape(SEQ // WIDTH, WIDTH), queries, keys, values, out_grad)
+    )(
+        segment_ids.reshape(SEQ // WIDTH, WIDTH),
+        queries,
+        keys.reshape(2, 2, HOME, WIDTH),
+        values.reshape(2, 2, HOME, WIDTH),
+        out_grad,
+    )
 
 
 def solution(mesh):

time: 75.2 us -> 62.3 us (0.83)
  the two profiles are of different devices: /device:TPU:25 before, /device:TPU:1 now
where the time goes in v4:
time: 62.3 us; the launch traced here: 61.5 us
  Pallas kernels  57.2 us (92%)
  local copies, waits for them, and re-layouts  3.65 us (6%)
  between operations  0.65 us (1%)
    pallas_call x1, Pallas kernels, on_device(): pl.pallas_call(kernel, out_shape=(tokens, tokens, terms, terms), in_specs...  57.2 us
    unnamed x10, local copies, waits for them, and re-layouts  3.65 us

profile of v4, /device:TPU:1, one launch (start us, length us, event | category | flops | bytes accessed | tf_op | source)
XLA Modules:
  0.0 61.5 jit_solution(12335619326530953533)
XLA Ops:
  0.6 57.2 %shard_map.84 = (bf16[256,256]{1,0:T(8,128)(2,1)}, bf16[256,256]{1,0:T(8,128)(2,1)}, bf16[64,128]{1,0:T(8,128)(2,1)}, bf16[64,128]{1,0:T(8,128)(2,1)}) custom-call(s32[64,128]{1,0:T(8,128)} %bitcast.5, bf16[256,1024]{1,0:T(8,128)(2,1)} %q_hbm.1, bf16[2,2,64,128]{3,2,1,0:T(8,128)(2,1)} %bitcast.3, bf16[2,2,64,128]{3,2,1,0:T(8,128)(2,1)} %bitcast.4, ...), custom_call_target="tpu_custom_call" | custom-call | tf_op jit(solution)/shard_map/pallas_call | solution.py:647
  57.9 0.0 copy-start
  57.9 1.6 %copy.13 = bf16[256,256]{1,0:T(8,128)(2,1)} copy(bf16[256,256]{1,0:T(8,128)(2,1)} %get-tuple-element.8) | data formatting | bytes 262144
  59.5 0.0 copy-done
  59.5 0.0 copy-start.2
  59.5 0.7 %copy.14 = bf16[256,256]{1,0:T(8,128)(2,1)} copy(bf16[256,256]{1,0:T(8,128)(2,1)S(1)} %copy-done) | data formatting | bytes 262144
  60.2 0.1 copy-done.2
  60.2 0.0 copy-start.1
  60.2 0.6 copy.15
  60.8 0.1 copy-done.1
  60.9 0.6 copy.16
Async XLA Ops:
  57.9 1.6 %copy-start = (bf16[256,256]{1,0:T(8,128)(2,1)S(1)}, bf16[256,256]{1,0:T(8,128)(2,1)}, u32[]{:S(2)}) copy-start(bf16[256,256]{1,0:T(8,128)(2,1)} %get-tuple-element.9) | copy-start | bytes 393220
  59.5 0.7 %copy-start.2 = (bf16[64,128]{1,0:T(8,128)(2,1)S(1)}, bf16[64,128]{1,0:T(8,128)(2,1)}, u32[]{:S(2)}) copy-start(bf16[64,128]{1,0:T(8,128)(2,1)} %get-tuple-element.10) | copy-start | bytes 49156
  60.2 0.7 %copy-start.1 = (bf16[64,128]{1,0:T(8,128)(2,1)S(1)}, bf16[64,128]{1,0:T(8,128)(2,1)}, u32[]{:S(2)}) copy-start(bf16[64,128]{1,0:T(8,128)(2,1)} %get-tuple-element.11) | copy-start | bytes 49156

commit v5 on v4

--- a/solution.py
+++ b/solution.py
@@ -19,9 +19,9 @@
 SEQ = PAIR * CHIPS
 GROUP = 128
 HOME = 64
-PER = 2
+PER = 4
 TILE = PER * GROUP
-TILES = 9
+TILES = 5
 HEADS = 2
 DEVS = 4
 NEG = -1e30
@@ -163,14 +163,13 @@
                     push(which, block, half, along("zy"[half], d2))
 
     def tile_in_order(n):
-        turn = n // 2
-        row_ = (y + jnp.where(turn == 2, 3, jnp.where(turn == 3, 2, turn))) % N
-        return 2 * row_ + n % 2
+        return (y + jnp.where(n == 2, 3, jnp.where(n == 3, 2, n))) % N
 
     def tile_arrived(which, b):
-        for j in (PER * b, PER * b + 1):
-            pl.when(j % N != z)(lambda j=j: arrived(which, j, 0))
-            pl.when(j // N != y)(lambda j=j: arrived(which, j, 1))
+        for i in range(PER):
+            j = PER * b + i
+            pl.when(z != i)(lambda j=j: arrived(which, j, 0))
+            pl.when(b != y)(lambda j=j: arrived(which, j, 1))
 
     def pair_copy(a):
         src, buf = arrays[a]
@@ -302,14 +301,14 @@
 
         return carry
 
-    lax.fori_loop(0, 2, scores_own, 0)
+    lax.fori_loop(0, 1, scores_own, 0)
     for copy in key_copies:
         copy.wait_send()
     kv_loads[1].wait()
     push_mine(1)
     share_own(1)
     pass_on(0)
-    lax.fori_loop(2, CHIPS // PER, scores_own, 0)
+    lax.fori_loop(1, CHIPS // PER, scores_own, 0)
     relay(1)
     share_pair(1)
     own_from_sibling(1)
@@ -323,15 +322,31 @@
 
     lax.fori_loop(0, n_other, scores_other, 0)
     pass_on(1)
-    lax.fori_loop(0, CHIPS // PER, lambda n, carry: (tile_arrived(1, tile_in_order(n)), carry)[1], 0)
-
-    def over_tiles(step):
-        def one(t, carry):
-            g = (t >= n_hi).astype(jnp.int32)
-            step(t, g, t - g * n_hi)
-            return carry
-
-        lax.fori_loop(0, TILES, one, 0)
+
+    def tile_place(t):
+        g = (t >= n_hi).astype(jnp.int32)
+        return g, t - g * n_hi
+
+    def weights_step(i, g, b):
+        t = b + g * n_hi
+        e = jnp.exp2(s_buf[i, t] - mx[i, g, 0:1])
+        tot[i, g] = tot[i, g] + fold(jnp.sum, e)
+        e = e.astype(BF16)
+        e_buf[i, t] = e
+        o = dot(tile_of(vall, b).T, e)
+        for r in (0, 1):
+            o_t[i, g, r] = o_t[i, g, r] + o[:, r * ROWS : (r + 1) * ROWS]
+
+    def weights_arriving(n, carry):
+        b = tile_in_order(n)
+        tile_arrived(1, b)
+        pl.when(b < n_hi)(lambda: weights_step(xp, 0, b))
+        pl.when(b < n_lo)(lambda: weights_step(xp, 1, b))
+        return carry
+
+    def weights_beside(n, carry):
+        weights_step(1 - xp, *tile_place(n))
+        return carry
 
     def statistics(i):
         for g in (0, 1):
@@ -345,24 +360,15 @@
         for slot, there in enumerate((beside(core), beside(1 - core), sibling)):
             go(remote(spot, spot, st_send.at[i, slot], st_recv.at[i, me], there))
 
-    for n, i in enumerate((xp, 1 - xp)):
+    for i in (0, 1):
         for g in (0, 1):
             mx[i, g] = jnp.broadcast_to(jnp.max(mx[i, g], axis=0, keepdims=True), (8, PAIR))
-
-        def weights_step(t, g, b, i=i):
-            e = jnp.exp2(s_buf[i, t] - mx[i, g, 0:1])
-            tot[i, g] = tot[i, g] + fold(jnp.sum, e)
-            e = e.astype(BF16)
-            e_buf[i, t] = e
-            o = dot(tile_of(vall, b).T, e)
-            for r in (0, 1):
-                o_t[i, g, r] = o_t[i, g, r] + o[:, r * ROWS : (r + 1) * ROWS]
-
-        over_tiles(weights_step)
-        if n == 0:
-            from_sibling(1)
-            turn_grads(1 - own)
-        statistics(i)
+    lax.fori_loop(0, CHIPS // PER, weights_arriving, 0)
+    from_sibling(1)
+    turn_grads(1 - own)
+    statistics(xp)
+    lax.fori_loop(0, TILES, weights_beside, 0)
+    statistics(1 - xp)
 
     ones = jnp.ones((TILE, WIDTH), BF16)
     sub = lax.broadcasted_iota(jnp.int32, (WIDTH, PAIR), 0)
@@ -461,7 +467,7 @@
             pl.when(needed)(lambda copy=copy: act(copy))
 
     def send_grads(b):
-        for j in (PER * b, PER * b + 1):
+        for j in [PER * b + k for k in range(PER)]:
             part[0, j] = (dkv[0, j] * scale).astype(BF16)
             part[1, j] = dkv[1, j].astype(BF16)
             each_first(j, lambda copy: copy.start())
@@ -479,15 +485,15 @@
             dq_t[i, g, r] = dq_t[i, g, r] + dq[:, r * ROWS : (r + 1) * ROWS]
 
     def grads_pass(i, leave):
-        def one(n, carry):
-            b = (2 * z + 2 + n) % (CHIPS // PER)
-            pl.when(b < n_hi)(lambda: grads_step(0, i, b))
-            pl.when(b < n_lo)(lambda: grads_step(1, i, b))
+        def one(t, carry):
+            g = (t < n_lo).astype(jnp.int32)
+            b = jnp.where(t < n_lo, t, (t - n_lo + z + 1) % n_hi)
+            grads_step(g, i, b)
             if leave:
-                pl.when(b < n_hi)(lambda: send_grads(b))
+                pl.when(g == 0)(lambda: send_grads(b))
             return carry
 
-        lax.fori_loop(0, CHIPS // PER, one, 0)
+        lax.fori_loop(0, TILES, one, 0)
         for g in (0, 1):
             to_core(1, i, g)
 
@@ -587,6 +593,11 @@
         copy.wait_send()
     for copy in stores:
         copy.wait()
+
+
+def hand_on(*refs):
+    for i in range(4):
+        refs[4 + i][...] = refs[i][...]
 
 
 def on_device(queries, keys, values, out_grad, segment_ids):
@@ -644,7 +655,7 @@
     ]
     tokens = jax.ShapeDtypeStruct((ROWS, 2 * WIDTH), BF16)
     terms = jax.ShapeDtypeStruct((HOME, WIDTH), BF16)
-    return pl.pallas_call(
+    parts = pl.pallas_call(
         kernel,
         out_shape=(tokens, tokens, terms, terms),
         in_specs=[hbm] * 5,
@@ -660,6 +671,12 @@
         values.reshape(2, 2, HOME, WIDTH),
         out_grad,
     )
+    return pl.pallas_call(
+        hand_on,
+        out_shape=(tokens, tokens, terms, terms),
+        in_specs=[pl.BlockSpec(memory_space=vmem)] * 4,
+        out_specs=(pl.BlockSpec(memory_space=vmem),) * 4,
+    )(*parts)
 
 
 def solution(mesh):

time: 62.3 us -> 57 us (0.915)
  local copies, waits for them, and re-layouts: 3.65 us -> 0 us
  Pallas kernels: 57.2 us -> 56 us
    unnamed x10 -> x0, local copies, waits for them, and re-layouts: 3.65 us -> none
    pallas_call x1, Pallas kernels: 57.2 us -> 54.3 us  [on_device(): pl.pallas_call(kernel, out_shape=(tokens, tokens, terms, terms), in_specs...]
    pallas_call x0 -> x1, Pallas kernels: none -> 1.69 us  [on_device(): pl.pallas_call(hand_on, out_shape=(tokens, tokens, terms, terms), in_spec...]
where the time goes in v5:
time: 57 us; the launch traced here: 56.6 us
  Pallas kernels  56 us (98%)
  between operations  0.64 us (1%)
    pallas_call x1, Pallas kernels, on_device(): pl.pallas_call(kernel, out_shape=(tokens, tokens, terms, terms), in_specs...  54.3 us
    pallas_call x1, Pallas kernels, on_device(): pl.pallas_call(hand_on, out_shape=(tokens, tokens, terms, terms), in_spec...  1.69 us

profile of v5, /device:TPU:1, one launch (start us, length us, event | category | flops | bytes accessed | tf_op | source)
XLA Modules:
  0.0 56.6 jit_solution(3780317762715596346)
XLA Ops:
  0.6 54.3 %shard_map.84 = (bf16[256,256]{1,0:T(8,128)(2,1)}, bf16[256,256]{1,0:T(8,128)(2,1)}, bf16[64,128]{1,0:T(8,128)(2,1)}, bf16[64,128]{1,0:T(8,128)(2,1)}) custom-call(s32[64,128]{1,0:T(8,128)} %bitcast.5, bf16[256,1024]{1,0:T(8,128)(2,1)} %q_hbm.1, bf16[2,2,64,128]{3,2,1,0:T(8,128)(2,1)} %bitcast.3, bf16[2,2,64,128]{3,2,1,0:T(8,128)(2,1)} %bitcast.4, ...), custom_call_target="tpu_custom_call" | custom-call | tf_op jit(solution)/shard_map/pallas_call | solution.py:658
  54.9 1.7 %shard_map.85 = (bf16[256,256]{1,0:T(8,128)(2,1)}, bf16[256,256]{1,0:T(8,128)(2,1)}, bf16[64,128]{1,0:T(8,128)(2,1)}, bf16[64,128]{1,0:T(8,128)(2,1)}) custom-call(bf16[256,256]{1,0:T(8,128)(2,1)} %get-tuple-element.8.refs_0_, bf16[256,256]{1,0:T(8,128)(2,1)} %get-tuple-element.9.refs_1_, bf16[64,128]{1,0:T(8,128)(2,1)} %get-tuple-element.10.refs_2_, ...), custom_call_target="tpu_custom_call" | custom-call | tf_op jit(solution)/shard_map/pallas_call | solution.py:674

commit v6 on v5

--- a/solution.py
+++ b/solution.py
@@ -33,12 +33,12 @@
 
 def kernel(
     seg_hbm, q_hbm, k_hbm, v_hbm, g_hbm,
-    out_hbm, dq_hbm, dk_hbm, dv_hbm,
+    out_ref, dq_ref, dk_ref, dv_ref,
     seg_ref, kall, vall, qbuf, gbuf, s_buf, e_buf,
     qa, gt, gpa, gp, mx, tot, o_t, dq_t, core_x, xs, xr, st, rng, dkv,
-    part, r1, d2, r2, d3, r3, acc, sums, final, obuf, orecv,
+    part, r1, d2, r2, d3, r3, acc, sums, obuf, orecv,
     load_sem, kv_sem, ag_send, ag_recv, pair_send, pair_recv, own_send, own_recv, x_send, x_recv, rel_send, rel_recv,
-    st_send, st_recv, core_send, core_recv, sum_send, sum_recv, out_send, out_recv, r1_send, r1_recv, r2_send, r2_recv, r3_send, r3_recv, store_sem,
+    st_send, st_recv, core_send, core_recv, sum_send, sum_recv, out_send, out_recv, r1_send, r1_recv, r2_send, r2_recv, r3_send, r3_recv,
 ):
     p = lax.axis_index("dp")
     c = lax.axis_index("ctx")
@@ -213,6 +213,8 @@
     share_own(0)
     go(pair_copy(1))
     relay(0)
+    kv_loads[1].wait()
+    push_mine(1)
 
     scale = WIDTH**-0.5
     seg_load.wait()
@@ -304,13 +306,11 @@
     lax.fori_loop(0, 1, scores_own, 0)
     for copy in key_copies:
         copy.wait_send()
-    kv_loads[1].wait()
-    push_mine(1)
     share_own(1)
+    share_pair(1)
     pass_on(0)
+    relay(1)
     lax.fori_loop(1, CHIPS // PER, scores_own, 0)
-    relay(1)
-    share_pair(1)
     own_from_sibling(1)
     turn_grads(own)
     from_sibling(0)
@@ -418,12 +418,6 @@
         xs[kind, g] = from_core(kind, 1 - xp, g).astype(BF16)
         go(remote(xs.at[kind, g], xr.at[kind, g], sum_send.at[kind, g], sum_recv.at[kind, g], beside(core)))
 
-    stores = []
-
-    def store(src, dst, i):
-        stores.append(pltpu.make_async_copy(src, dst, store_sem.at[i]))
-        stores[-1].start()
-
     def finish(kind, g):
         total = from_core(kind, xp, g)
         spot = xr.at[kind, g]
@@ -435,7 +429,7 @@
 
     def finish_own(kind):
         finish(kind, own)
-        store(obuf.at[kind, own], (out_hbm, dq_hbm)[kind].at[:, cols(upper)], kind)
+        (out_ref, dq_ref)[kind][:, cols(upper)] = obuf[kind, own]
 
     def partner_copy(kind):
         return remote(obuf.at[kind, 1 - own], orecv.at[kind], out_send.at[kind], out_recv.at[kind], partner)
@@ -446,7 +440,7 @@
 
     def from_partner(kind):
         partner_copy(kind).wait_recv()
-        store(orecv.at[kind], (out_hbm, dq_hbm)[kind].at[:, cols(1 - upper)], 2 + kind)
+        (out_ref, dq_ref)[kind][:, cols(1 - upper)] = orecv[kind]
 
     def touched(k, j):
         return j // PER <= upper_of(k) // PER
@@ -485,15 +479,23 @@
             dq_t[i, g, r] = dq_t[i, g, r] + dq[:, r * ROWS : (r + 1) * ROWS]
 
     def grads_pass(i, leave):
-        def one(t, carry):
-            g = (t < n_lo).astype(jnp.int32)
-            b = jnp.where(t < n_lo, t, (t - n_lo + z + 1) % n_hi)
-            grads_step(g, i, b)
-            if leave:
-                pl.when(g == 0)(lambda: send_grads(b))
+        def lower(b, carry):
+            grads_step(1, i, b)
             return carry
 
-        lax.fori_loop(0, TILES, one, 0)
+        def upper_tile(n, carry):
+            b = (z + 1 + n) % N
+
+            @pl.when(b < n_hi)
+            def _():
+                grads_step(0, i, b)
+                if leave:
+                    send_grads(b)
+
+            return carry
+
+        lax.fori_loop(0, n_lo, lower, 0)
+        lax.fori_loop(0, N, upper_tile, 0)
         for g in (0, 1):
             to_core(1, i, g)
 
@@ -568,9 +570,8 @@
             remote(spot, spot, r3_send.at[0], r3_recv.at[u], sibling).wait_recv()
             sums[...] = sums[...] + r3[u].astype(F32)
 
-    final[...] = sums[...].astype(BF16)
-    store(final.at[0], dk_hbm, 4)
-    store(final.at[1], dv_hbm, 5)
+    for which, ref in enumerate((dk_ref, dv_ref)):
+        ref[...] = sums[which].astype(BF16)
     from_partner(0)
     from_partner(1)
 
@@ -591,8 +592,6 @@
         pl.when(needed)(lambda copy=copy: copy.wait_send())
     for copy in started:
         copy.wait_send()
-    for copy in stores:
-        copy.wait()
 
 
 def hand_on(*refs):
@@ -634,7 +633,6 @@
         vmem((2, 2, HOME, WIDTH), BF16),
         vmem((GROUP, WIDTH), F32),
         vmem((2, HOME, WIDTH), F32),
-        vmem((2, HOME, WIDTH), BF16),
         vmem((2, 2, ROWS, WIDTH), BF16),
         vmem((2, ROWS, WIDTH), BF16),
         dma((2, HEADS)),
@@ -651,15 +649,15 @@
         dma((2, CHIPS)), dma((2, N - 1, N)),
         dma((2, N)), dma((2, N - 1)),
         dma((2,)), dma((2,)),
-        dma((6,)),
     ]
     tokens = jax.ShapeDtypeStruct((ROWS, 2 * WIDTH), BF16)
     terms = jax.ShapeDtypeStruct((HOME, WIDTH), BF16)
+    results = (tokens, tokens, terms, terms)
     parts = pl.pallas_call(
         kernel,
-        out_shape=(tokens, tokens, terms, terms),
+        out_shape=[vmem(like.shape, like.dtype) for like in results],
         in_specs=[hbm] * 5,
-        out_specs=(hbm,) * 4,
+        out_specs=[pl.BlockSpec(memory_space=vmem)] * 4,
         scratch_shapes=scratch,
         compiler_params=pltpu.CompilerParams(
             collective_id=0, has_side_effects=True, vmem_limit_bytes=56 * 1024 * 1024
@@ -673,10 +671,10 @@
     )
     return pl.pallas_call(
         hand_on,
-        out_shape=(tokens, tokens, terms, terms),
+        out_shape=results,
         in_specs=[pl.BlockSpec(memory_space=vmem)] * 4,
         out_specs=(pl.BlockSpec(memory_space=vmem),) * 4,
-    )(*parts)
+    )(*[pltpu.with_memory_space_constraint(part, vmem) for part in parts])
 
 
 def solution(mesh):

time: 57 us -> 54.6 us (0.958)
  Pallas kernels: 56 us -> 53.4 us
    pallas_call x2, Pallas kernels: 56 us -> 53.4 us  [the longest x1 52.7 us: on_device(): pl.pallas_call(kernel, out_shape=[vmem(like.shape, like.dtype) for like i...]
where the time goes in v6:
time: 54.6 us; the launch traced here: 54 us
  Pallas kernels  53.4 us (98%)
  between operations  0.64 us (1%)
    pallas_call x1, Pallas kernels, on_device(): pl.pallas_call(kernel, out_shape=[vmem(like.shape, like.dtype) for like i...  52.7 us

profile of v6, /device:TPU:1, one launch (start us, length us, event | category | flops | bytes accessed | tf_op | source)
XLA Modules:
  0.0 54.0 jit_solution(1290069810199996694)
XLA Ops:
  0.6 52.7 %shard_map.84 = (bf16[256,256]{1,0:T(8,128)(2,1)S(1)}, bf16[256,256]{1,0:T(8,128)(2,1)S(1)}, bf16[64,128]{1,0:T(8,128)(2,1)S(1)}, bf16[64,128]{1,0:T(8,128)(2,1)S(1)}) custom-call(s32[64,128]{1,0:T(8,128)} %bitcast.5, bf16[256,1024]{1,0:T(8,128)(2,1)} %q_hbm.1, bf16[2,2,64,128]{3,2,1,0:T(8,128)(2,1)} %bitcast.3, bf16[2,2,64,128]{3,2,1,0:T(8,128)(2,1)} %bitcast.4, ...), custom_call_target="tpu_custom_call" | custom-call | tf_op jit(solution)/shard_map/pallas_call | solution.py:656
  53.3 0.7 %shard_map.85 = (bf16[256,256]{1,0:T(8,128)(2,1)}, bf16[256,256]{1,0:T(8,128)(2,1)}, bf16[64,128]{1,0:T(8,128)(2,1)}, bf16[64,128]{1,0:T(8,128)(2,1)}) custom-call(bf16[256,256]{1,0:T(8,128)(2,1)S(1)} %get-tuple-element.8.refs_0_, bf16[256,256]{1,0:T(8,128)(2,1)S(1)} %get-tuple-element.9.refs_1_, bf16[64,128]{1,0:T(8,128)(2,1)S(1)} %get-tuple-element.10.refs_2_, ...), custom_call_target="tpu_custom_call" | custom-call | tf_op jit(solution)/shard_map/pallas_call | solution.py:672

commit v7 on v6

--- a/solution.py
+++ b/solution.py
@@ -495,6 +495,9 @@
             return carry
 
         lax.fori_loop(0, n_lo, lower, 0)
+        if leave:
+            for g in (0, 1):
+                to_beside(1, g)
         lax.fori_loop(0, N, upper_tile, 0)
         for g in (0, 1):
             to_core(1, i, g)
@@ -506,9 +509,8 @@
     prepare(xp)
     for g in (0, 1):
         to_core(0, xp, g)
-    for kind in (0, 1):
-        for g in (0, 1):
-            to_beside(kind, g)
+    for g in (0, 1):
+        to_beside(0, g)
     grads_pass(xp, True)
 
     def second_copy(which, i):
@@ -539,6 +541,7 @@
 
     lax.fori_loop(0, N, first_sum, 0)
     finish_other(1)
+    finish_other(0)
     for which, i in ((0, z), (1, y)):
         total = d2[which, i].astype(F32)
         for s in range(N - 1):
@@ -558,7 +561,6 @@
         copy, needed = third_copy(half)
         pl.when(needed)(lambda copy=copy: copy.start())
     finish_own(1)
-    finish_other(0)
     finish_own(0)
     total = jnp.where(keeps, d3[core].astype(F32), 0.0)
     sums[...] = total

time: 54.6 us -> 53.5 us (0.980)
  Pallas kernels: 53.4 us -> 52.7 us
    pallas_call x1, Pallas kernels: 52.7 us -> 52 us  [on_device(): pl.pallas_call(kernel, out_shape=[vmem(like.shape, like.dtype) for like i...]
where the time goes in v7:
time: 53.5 us; the launch traced here: 53.4 us
  Pallas kernels  52.7 us (99%)
  between operations  0.64 us (1%)
    pallas_call x1, Pallas kernels, on_device(): pl.pallas_call(kernel, out_shape=[vmem(like.shape, like.dtype) for like i...  52 us

profile of v7, /device:TPU:1, one launch (start us, length us, event | category | flops | bytes accessed | tf_op | source)
XLA Modules:
  0.0 53.4 jit_solution(3136498731167538356)
XLA Ops:
  0.6 52.0 %shard_map.84 = (bf16[256,256]{1,0:T(8,128)(2,1)S(1)}, bf16[256,256]{1,0:T(8,128)(2,1)S(1)}, bf16[64,128]{1,0:T(8,128)(2,1)S(1)}, bf16[64,128]{1,0:T(8,128)(2,1)S(1)}) custom-call(s32[64,128]{1,0:T(8,128)} %bitcast.5, bf16[256,1024]{1,0:T(8,128)(2,1)} %q_hbm.1, bf16[2,2,64,128]{3,2,1,0:T(8,128)(2,1)} %bitcast.3, bf16[2,2,64,128]{3,2,1,0:T(8,128)(2,1)} %bitcast.4, ...), custom_call_target="tpu_custom_call" | custom-call | tf_op jit(solution)/shard_map/pallas_call | solution.py:658
  52.6 0.7 %shard_map.85 = (bf16[256,256]{1,0:T(8,128)(2,1)}, bf16[256,256]{1,0:T(8,128)(2,1)}, bf16[64,128]{1,0:T(8,128)(2,1)}, bf16[64,128]{1,0:T(8,128)(2,1)}) custom-call(bf16[256,256]{1,0:T(8,128)(2,1)S(1)} %get-tuple-element.8.refs_0_, bf16[256,256]{1,0:T(8,128)(2,1)S(1)} %get-tuple-element.9.refs_1_, bf16[64,128]{1,0:T(8,128)(2,1)S(1)} %get-tuple-element.10.refs_2_, ...), custom_call_target="tpu_custom_call" | custom-call | tf_op jit(solution)/shard_map/pallas_call | solution.py:674

commit v8 on v7

--- a/solution.py
+++ b/solution.py
@@ -449,8 +449,9 @@
         axis = "yz"[which]
         d = (j % N + N - y) % N if which == 0 else (j // N + N - z) % N
         index = j // N if which == 0 else j % N
+        slot = jnp.maximum(d - 1, 0)
         copy = remote(
-            part.at[which, j], r1.at[which, d - 1, index], r1_send.at[which, j], r1_recv.at[which, d - 1, index],
+            part.at[which, j], r1.at[which, slot, index], r1_send.at[which, j], r1_recv.at[which, slot, index],
             along(axis, d),
         )
         return copy, d != 0
@@ -515,8 +516,9 @@
 
     def second_copy(which, i):
         d = (i + N - (z if which == 0 else y)) % N
+        slot = jnp.maximum(d - 1, 0)
         copy = remote(
-            d2.at[which, i], r2.at[which, d - 1], r2_send.at[which, i], r2_recv.at[which, d - 1],
+            d2.at[which, i], r2.at[which, slot], r2_send.at[which, i], r2_recv.at[which, slot],
             along("zy"[which], d),
         )
         return copy, d != 0

time: 53.5 us -> 53.5 us (level)
  no operation moved by 1% of the time
where the time goes in v8:
time: 53.5 us; the launch traced here: 53.4 us
  Pallas kernels  52.7 us (99%)
  between operations  0.64 us (1%)
    pallas_call x1, Pallas kernels, on_device(): pl.pallas_call(kernel, out_shape=[vmem(like.shape, like.dtype) for like i...  52 us

profile of v8, /device:TPU:1, one launch (start us, length us, event | category | flops | bytes accessed | tf_op | source)
XLA Modules:
  0.0 53.4 jit_solution(10201703492715497023)
XLA Ops:
  0.6 52.0 %shard_map.84 = (bf16[256,256]{1,0:T(8,128)(2,1)S(1)}, bf16[256,256]{1,0:T(8,128)(2,1)S(1)}, bf16[64,128]{1,0:T(8,128)(2,1)S(1)}, bf16[64,128]{1,0:T(8,128)(2,1)S(1)}) custom-call(s32[64,128]{1,0:T(8,128)} %bitcast.5, bf16[256,1024]{1,0:T(8,128)(2,1)} %q_hbm.1, bf16[2,2,64,128]{3,2,1,0:T(8,128)(2,1)} %bitcast.3, bf16[2,2,64,128]{3,2,1,0:T(8,128)(2,1)} %bitcast.4, ...), custom_call_target="tpu_custom_call" | custom-call | tf_op jit(solution)/shard_map/pallas_call | solution.py:660
  52.6 0.7 %shard_map.85 = (bf16[256,256]{1,0:T(8,128)(2,1)}, bf16[256,256]{1,0:T(8,128)(2,1)}, bf16[64,128]{1,0:T(8,128)(2,1)}, bf16[64,128]{1,0:T(8,128)(2,1)}) custom-call(bf16[256,256]{1,0:T(8,128)(2,1)S(1)} %get-tuple-element.8.refs_0_, bf16[256,256]{1,0:T(8,128)(2,1)S(1)} %get-tuple-element.9.refs_1_, bf16[64,128]{1,0:T(8,128)(2,1)S(1)} %get-tuple-element.10.refs_2_, ...), custom_call_target="tpu_custom_call" | custom-call | tf_op jit(solution)/shard_map/pallas_call | solution.py:676

commit v9 on v8

--- a/solution.py
+++ b/solution.py
@@ -496,12 +496,12 @@
             return carry
 
         lax.fori_loop(0, n_lo, lower, 0)
+        to_core(1, i, 1)
         if leave:
             for g in (0, 1):
                 to_beside(1, g)
         lax.fori_loop(0, N, upper_tile, 0)
-        for g in (0, 1):
-            to_core(1, i, g)
+        to_core(1, i, 0)
 
     prepare(1 - xp)
     for g in (0, 1):

time: 53.5 us -> 53.4 us (level)
  no operation moved by 1% of the time
where the time goes in v9:
time: 53.4 us; the launch traced here: 53.3 us
  Pallas kernels  52.6 us (99%)
  between operations  0.64 us (1%)
    pallas_call x1, Pallas kernels, on_device(): pl.pallas_call(kernel, out_shape=[vmem(like.shape, like.dtype) for like i...  51.9 us

profile of v9, /device:TPU:1, one launch (start us, length us, event | category | flops | bytes accessed | tf_op | source)
XLA Modules:
  0.0 53.3 jit_solution(558453763983588058)
XLA Ops:
  0.6 51.9 %shard_map.84 = (bf16[256,256]{1,0:T(8,128)(2,1)S(1)}, bf16[256,256]{1,0:T(8,128)(2,1)S(1)}, bf16[64,128]{1,0:T(8,128)(2,1)S(1)}, bf16[64,128]{1,0:T(8,128)(2,1)S(1)}) custom-call(s32[64,128]{1,0:T(8,128)} %bitcast.5, bf16[256,1024]{1,0:T(8,128)(2,1)} %q_hbm.1, bf16[2,2,64,128]{3,2,1,0:T(8,128)(2,1)} %bitcast.3, bf16[2,2,64,128]{3,2,1,0:T(8,128)(2,1)} %bitcast.4, ...), custom_call_target="tpu_custom_call" | custom-call | tf_op jit(solution)/shard_map/pallas_call | solution.py:660
  52.6 0.7 %shard_map.85 = (bf16[256,256]{1,0:T(8,128)(2,1)}, bf16[256,256]{1,0:T(8,128)(2,1)}, bf16[64,128]{1,0:T(8,128)(2,1)}, bf16[64,128]{1,0:T(8,128)(2,1)}) custom-call(bf16[256,256]{1,0:T(8,128)(2,1)S(1)} %get-tuple-element.8.refs_0_, bf16[256,256]{1,0:T(8,128)(2,1)S(1)} %get-tuple-element.9.refs_1_, bf16[64,128]{1,0:T(8,128)(2,1)S(1)} %get-tuple-element.10.refs_2_, ...), custom_call_target="tpu_custom_call" | custom-call | tf_op jit(solution)/shard_map/pallas_call | solution.py:676
